TPU v7x, 32 devices: a whole 2x2x4 slice. The times are simulated.
32 devices in a mesh: dp: 8 (over y, x, core), seq: 4 (over z).
Axes of the slice: x: 2, y: 2, z: 4, core: 2. Of those that a mesh axis runs over, the one named last changes fastest.
Arguments:
- patches: bfloat16 [24, 532, 768], P('dp', 'seq'), may hold values from -6 to 6
- cotangent: bfloat16 [24, 532, 768], P('dp', 'seq'), may hold values from -6 to 6
- lengths: int32 [24], P('dp'), may hold values from 66 to 529, as said below
- script_ids: int32 [24], P('dp'), may hold values from 0 to 1, as said below
- key_mask: int32 [24, 532], P('dp'), may hold values 0 or 1
- norm1_gain: bfloat16 [768], P(('dp', 'seq')), may hold values from 0.5 to 1.5
- norm1_bias: bfloat16 [768], P(('dp', 'seq')), may hold values from -1 to 1
- w_qkv: bfloat16 [768, 2304], P(('dp', 'seq')), may hold values from -0.21875 to 0.21875
- q_bias: bfloat16 [768], P(('dp', 'seq')), may hold values from -1 to 1
- v_bias: bfloat16 [768], P(('dp', 'seq')), may hold values from -1 to 1
- w_attn_out: bfloat16 [768, 768], P(('dp', 'seq')), may hold values from -2.5 to 2.5
- attn_out_bias: bfloat16 [768], P(('dp', 'seq')), may hold values from -1 to 1
- norm2_gain: bfloat16 [768], P(('dp', 'seq')), may hold values from 0.5 to 1.5
- norm2_bias: bfloat16 [768], P(('dp', 'seq')), may hold values from -1 to 1
- w_up: bfloat16 [768, 3072], P(('dp', 'seq')), may hold values from -0.21875 to 0.21875
- up_bias: bfloat16 [3072], P(('dp', 'seq')), may hold values from -1 to 1
- w_down: bfloat16 [3072, 768], P(('dp', 'seq')), may hold values from -0.109375 to 0.109375
- down_bias: bfloat16 [768], P(('dp', 'seq')), may hold values from -1 to 1
- script_table: bfloat16 [2, 768], P(None, ('dp', 'seq')), may hold values from -3 to 3
Outputs:
- block_out: bfloat16 [24, 532, 768], P('dp', 'seq')
- input_grad: bfloat16 [24, 532, 768], P('dp', 'seq')
- grad_norm1_gain: float32 [768], P(('dp', 'seq'))
- grad_norm1_bias: float32 [768], P(('dp', 'seq'))
- grad_w_qkv: float32 [768, 2304], P(('dp', 'seq'))
- grad_q_bias: float32 [768], P(('dp', 'seq'))
- grad_v_bias: float32 [768], P(('dp', 'seq'))
- grad_w_attn_out: float32 [768, 768], P(('dp', 'seq'))
- grad_attn_out_bias: float32 [768], P(('dp', 'seq'))
- grad_norm2_gain: float32 [768], P(('dp', 'seq'))
- grad_norm2_bias: float32 [768], P(('dp', 'seq'))
- grad_w_up: float32 [768, 3072], P(('dp', 'seq'))
- grad_up_bias: float32 [3072], P(('dp', 'seq'))
- grad_w_down: float32 [3072, 768], P(('dp', 'seq'))
- grad_down_bias: float32 [768], P(('dp', 'seq'))
- grad_script_table: float32 [2, 768], P(None, ('dp', 'seq'))
Inputs may be any that keep to these rules, and one draw needn't show every extreme that they name: `lengths`: a strip of a dense script (script_ids 1) holds 396 to 529 patches, a strip of a sparse one (script_ids 0) * 529 // 8 to 264; some strip has exactly 529. `script_ids`: 1 marks a strip of a dense script, 0 a sparse one.
All inputs are finite; a program needn't handle non-finite values. No bound on the sum of `key_mask` on one device may be relied on, other than what follows from the above.
Results may differ from a plain program's by a relative error of at most 0.012.
Values may be sent and summed in bfloat16 or wider, within the bound.
A program may use at most 128 MiB of HBM per device.

v0:
```python
import functools

import jax
import jax.numpy as jnp
from jax import lax
from jax.experimental import pallas as pl
from jax.experimental.pallas import tpu as pltpu
from jax.sharding import PartitionSpec as P

DH = 64
MESH = pl.DeviceIdType.MESH
f32 = jnp.float32
bf16 = jnp.bfloat16
epsilon = 1e-06
WIRE = 12
HOPS = 8
QKV, OUT, UP = 0, 3, 4
G1, B1, QB, VB, OB, G2, B2, DB, T0, T1 = range(10)


def round_up(n, m):
    return (n + m - 1) // m * m


def ds(start, size, align=16):
    return pl.ds(pl.multiple_of(start, align), size)


def nn(a, b):
    return lax.dot_general(a, b, (((1,), (0,)), ((), ())), preferred_element_type=f32)


def nt(a, b):
    return lax.dot_general(a, b, (((1,), (1,)), ((), ())), preferred_element_type=f32)


def tn(a, b):
    return lax.dot_general(a, b, (((0,), (0,)), ((), ())), preferred_element_type=f32)


def loop(n, body):
    def step(i, carry):
        body(i)
        return carry

    lax.fori_loop(0, n, step, 0)


def total(v):
    return jnp.sum(v, axis=0, keepdims=True)


def remote(src, dst, send, recv, to):
    return pltpu.make_async_remote_copy(
        src_ref=src, dst_ref=dst, send_sem=send, recv_sem=recv, device_id=to, device_id_type=MESH
    )


class Place:
    def __init__(self, outer, groups):
        self.dp = lax.axis_index("dp")
        self.z = lax.axis_index("seq")
        self.groups = groups
        b = self.dp // outer
        self.c = b % 2
        self.x = (b // 2) % 2
        self.y = b // 4
        self.to_c = (self.dp + outer * (1 - 2 * self.c), self.z)
        self.to_x = (self.dp + outer * (2 - 4 * self.x), self.z)
        self.to_y = (self.dp + outer * (4 - 8 * self.y), self.z)

    def ahead(self, j):
        return (self.z + j) % self.groups

    def behind(self, j):
        return (self.z + self.groups - j) % self.groups

    def to_z(self, z):
        return (self.dp, z)

    def greet(self):
        barrier = pltpu.get_barrier_semaphore()
        peers = [self.to_c, self.to_x, self.to_y]
        peers += [self.to_z(self.ahead(j)) for j in range(1, self.groups)]
        for peer in peers:
            pl.semaphore_signal(barrier, inc=1, device_id=peer, device_id_type=MESH)
        pl.semaphore_wait(barrier, len(peers))


class Gather:
    def __init__(self, place, index, shard, block, part, land, send, recv, settle=None):
        self.p, self.i, self.shard = place, index, shard
        self.block, self.part, self.land, self.settle = block, part, land, settle
        self.send, self.recv = send, recv

    def copy(self, k, ref, to):
        return remote(ref, ref, self.send.at[self.i, k], self.recv.at[self.i, k], to)

    def z_copy(self, j, owner):
        return remote(
            self.shard, self.land(owner), self.send.at[self.i, j - 1], self.recv.at[self.i, j - 1],
            self.p.to_z(self.p.ahead(j)),
        )

    def z_start(self):
        p = self.p
        for j in range(1, p.groups):
            self.z_copy(j, p.z).start()
        self.land(p.z)[...] = self.shard[...]

    def xy(self, k):
        p = self.p
        mx, my = 1 - p.x, 1 - p.y
        own = lambda: self.block(p.y, p.x, p.c)
        bx = lambda: self.block(p.y, mx, p.c)
        by = lambda: self.block(my, p.x, p.c)
        bd = lambda: self.block(my, mx, p.c)
        if k == 3:
            return self.copy(3, own(), p.to_x)
        if k == 4:
            return self.copy(4, own(), p.to_y)
        if k == 5:
            return self.copy(5, self.part(by(), 1), p.to_x)
        if k == 6:
            return self.copy(6, self.part(bx(), 0), p.to_y)
        if k == 7:
            return self.copy(7, own(), p.to_c)
        if k == 8:
            return self.copy(8, bx(), p.to_c)
        if k == 9:
            return self.copy(9, by(), p.to_c)
        return self.copy(k, self.part(bd(), k - 10), p.to_c)

    def z_finish(self):
        p = self.p
        for j in range(1, p.groups):
            self.z_copy(j, p.behind(j)).wait_recv()
        if self.settle is not None:
            self.settle(self.block(p.y, p.x, p.c))
        for k in (3, 4, 7):
            self.xy(k).start()

    def mid(self):
        self.xy(3).wait_recv()
        self.xy(6).start()
        self.xy(8).start()
        self.xy(4).wait_recv()
        self.xy(5).start()
        self.xy(9).start()

    def diag(self):
        self.xy(6).wait_recv()
        self.xy(10).start()
        self.xy(5).wait_recv()
        self.xy(11).start()

    def finish(self):
        p = self.p
        for k in (7, 8, 9, 10, 11):
            self.xy(k).wait_recv()
        for j in range(1, p.groups):
            self.z_copy(j, p.z).wait_send()
        for k in range(3, WIRE):
            self.xy(k).wait_send()


class Rows:
    def __init__(self, place, parts, strip, send, recv):
        self.p, self.parts, self.strip, self.send, self.recv = place, parts, strip, send, recv
        self.strips, self.rows = parts.shape[0], parts.shape[1]
        self.home = place.z - place.c
        self.is_home = (self.home >= 0) & (self.home < self.strips)

    def clip(self, s):
        return jnp.clip(s, 0, self.strips - 1)

    def at(self, z):
        return self.strip.at[ds(z * self.rows, self.rows)]

    def inward(self, j, owner, s):
        return remote(
            self.parts.at[s], self.at(owner), self.send.at[j - 1], self.recv.at[j - 1],
            self.p.to_z(self.p.ahead(j)),
        )

    def in_start(self):
        p = self.p
        for j in range(1, p.groups):
            s = p.ahead(j) - p.c

            @pl.when((s >= 0) & (s < self.strips))
            def _():
                self.inward(j, p.z, self.clip(s)).start()

        @pl.when(self.is_home)
        def _():
            self.strip[ds(p.z * self.rows, self.rows), :] = self.parts[self.clip(self.home)]

        @pl.when(jnp.logical_not(self.is_home))
        def _():
            self.strip[...] = jnp.zeros_like(self.strip)

    def in_finish(self):
        p = self.p

        @pl.when(self.is_home)
        def _():
            for j in range(1, p.groups):
                self.inward(j, p.behind(j), 0).wait_recv()

    def in_sent(self):
        p = self.p
        for j in range(1, p.groups):
            s = p.ahead(j) - p.c

            @pl.when((s >= 0) & (s < self.strips))
            def _():
                self.inward(j, p.z, self.clip(s)).wait_send()

    def outward(self, j, s):
        z = self.p.ahead(j)
        return remote(
            self.at(z), self.parts.at[s], self.send.at[j - 1], self.recv.at[j - 1], self.p.to_z(z)
        )

    def out_start(self):
        p = self.p

        @pl.when(self.is_home)
        def _():
            home = self.clip(self.home)
            for j in range(1, p.groups):
                self.outward(j, home).start()
            self.parts[home] = self.strip[ds(p.z * self.rows, self.rows), :]

    def out_finish(self):
        p = self.p
        for j in range(1, p.groups):
            s = p.behind(j) - p.c

            @pl.when((s >= 0) & (s < self.strips))
            def _():
                self.outward(j, self.clip(s)).wait_recv()

        @pl.when(self.is_home)
        def _():
            for j in range(1, p.groups):
                self.outward(j, self.clip(self.home)).wait_send()


def add_into(dst, terms, rows, step=48):
    def body(i):
        at = ds(i * step, step)
        value = terms[0][at, :]
        for term in terms[1:]:
            value = value + term[at, :]
        dst[at, :] = value

    loop(rows // step, body)


class Scatter:
    def __init__(self, place, index, part, bufs, out, send, recv):
        self.p, self.i, self.part = place, index, part
        self.core, self.r1, self.r2, self.q1, self.q2, self.zs, self.zr = bufs
        self.out, self.send, self.recv = out, send, recv
        self.k, self.u, self.n = self.q1.shape[0], self.core.shape[3], self.q1.shape[2]
        self.r = self.u // place.groups
        self.first, self.second = pl.ds(0, self.u // 2), pl.ds(self.u // 2, self.u // 2)

    def wire(self, k):
        p, i = self.p, self.i
        if k == 0:
            src, dst, to = self.part.at[:, :, :, 1 - p.c], self.core, p.to_c
        elif k == 1:
            src, dst, to = self.core.at[:, :, 1 - p.x, self.first], self.r1, p.to_x
        elif k == 2:
            src, dst, to = self.core.at[:, 1 - p.y, :, self.second], self.r2, p.to_y
        elif k == 3:
            src, dst, to = self.r1.at[:, 1 - p.y], self.q1, p.to_y
        elif k == 4:
            src, dst, to = self.r2.at[:, 1 - p.x], self.q2, p.to_x
        else:
            z = p.ahead(k - 4)
            src, dst, to = self.zs.at[:, z], self.zr.at[k - 5], p.to_z(z)
        return remote(src, dst, self.send.at[i, k], self.recv.at[i, k], to)

    def start(self):
        self.wire(0).start()

    def core_add(self):
        p = self.p
        self.wire(0).wait_recv()
        for k in range(self.k):
            for y in range(2):
                for x in range(2):
                    here = self.core.at[k, y, x]
                    add_into(here, (here, self.part.at[k, y, x, p.c]), self.u)
        self.wire(1).start()
        self.wire(2).start()

    def pass_on(self):
        p = self.p
        self.wire(1).wait_recv()
        for k in range(self.k):
            here = self.r1.at[k, 1 - p.y]
            add_into(here, (here, self.core.at[k, 1 - p.y, p.x, self.first]), self.u // 2)
        self.wire(3).start()
        self.wire(2).wait_recv()
        for k in range(self.k):
            here = self.r2.at[k, 1 - p.x]
            add_into(here, (here, self.core.at[k, p.y, 1 - p.x, self.second]), self.u // 2)
        self.wire(4).start()

    def z_start(self):
        p, r = self.p, self.r
        half = self.u // 2
        self.wire(3).wait_recv()
        self.wire(4).wait_recv()
        per = p.groups // 2
        for k in range(self.k):
            for h in range(2):
                mine = self.r1.at[k, p.y] if h == 0 else self.r2.at[k, p.x]
                got = self.q1.at[k] if h == 0 else self.q2.at[k]
                value = self.core[k, p.y, p.x, pl.ds(h * half, half), :].astype(f32)
                value += mine[...].astype(f32) + got[...].astype(f32)
                slabs = value.reshape(per, r, self.n)
                self.zs[k, pl.ds(h * per, per)] = slabs.astype(bf16)
        for j in range(1, p.groups):
            self.wire(4 + j).start()

    def finish(self):
        p = self.p
        for j in range(1, p.groups):
            self.wire(4 + j).wait_recv()
        for k in range(self.k):
            value = self.zs[k, p.z].astype(f32)
            for j in range(1, p.groups):
                value += self.zr[j - 1, k].astype(f32)
            self.out[k][...] = value

    def drain(self):
        for k in range(HOPS):
            self.wire(k).wait_send()


class Tally:
    def __init__(self, place, value, got, send, recv):
        self.p, self.value, self.got, self.send, self.recv = place, value, got, send, recv

    def copy(self, k):
        p = self.p
        to = (p.to_c, p.to_x, p.to_y)[k] if k < 3 else p.to_z(p.ahead(k - 2))
        return remote(
            self.value.at[min(k, 3)], self.got.at[k], self.send.at[k], self.recv.at[k], to
        )

    def start(self):
        self.copy(0).start()

    def step(self, k):
        self.copy(k).wait_recv()
        self.value[k + 1] = self.value[k] + self.got[k]
        if k < 2:
            self.copy(k + 1).start()
        else:
            for j in range(1, self.p.groups):
                self.copy(2 + j).start()

    def finish(self):
        value = self.value[3]
        for j in range(1, self.p.groups):
            self.copy(2 + j).wait_recv()
            value += self.got[2 + j]
        for k in range(2 + self.p.groups):
            self.copy(k).wait_send()
        return value


def normalize(v):
    mean = jnp.mean(v, axis=1, keepdims=True)
    centred = v - mean
    inv = lax.rsqrt(jnp.mean(centred * centred, axis=1, keepdims=True) + epsilon)
    return centred * inv, mean, inv


def norm_backward(grad, hat, inv, gain):
    t = grad * gain
    mean_t = jnp.mean(t, axis=1, keepdims=True)
    mean_th = jnp.mean(t * hat, axis=1, keepdims=True)
    return inv * (t - mean_t - hat * mean_th)


class Layer:
    def __init__(self, place, refs):
        self.__dict__.update(refs)
        self.p = place
        self.rows, self.d = self.x.shape
        self.hidden = self.act.shape[1]
        self.step = 96

    def vec(self, i):
        return self.vecs[i : i + 1, :]

    def weight(self, i, cols=slice(None)):
        value = self.w[i, :, :, :, :, cols]
        return value.reshape(self.d, value.shape[-1])

    def eighths(self, value):
        return value.reshape(2, 2, 2, value.shape[0] // 8, value.shape[1])

    def vectors(self):
        d, groups = self.d, self.p.groups
        per = d // (8 * groups)
        wide = self.hidden // (8 * groups)

        def spread(lanes, cols, width):
            lane = lax.broadcasted_iota(jnp.int32, (lanes, cols), 0)
            col = lax.broadcasted_iota(jnp.int32, (lanes, cols), 1)
            hit = (col == lane // 128 * width + lane % 128) & (lane % 128 < width)
            return jnp.where(hit, 1.0, 0.0).astype(bf16)

        half = spread(4 * groups * 128, d // 2, per)
        for h in range(2):
            slabs = [self.small[4 * h + b, z] for b in range(4) for z in range(groups)]
            self.vecs[:, h * (d // 2) : (h + 1) * (d // 2)] = nn(jnp.concatenate(slabs, 1), half)
        one = spread(groups * 128, groups * wide, wide)
        for b in range(8):
            slabs = [self.small[b, z] for z in range(groups)]
            row = nn(jnp.concatenate(slabs, 1), one)[10:11, :]
            self.b_up[:, b * groups * wide : (b + 1) * groups * wide] = row

    def mask(self, lengths, script_ids, key_mask):
        strips, length = key_mask.shape
        home = jnp.clip(self.p.z - self.p.c, 0, strips - 1)
        keys = jnp.zeros((1, length), jnp.int32)
        for s in range(strips):
            keys = jnp.where(home == s, key_mask[s : s + 1, :], keys)
        pos = lax.broadcasted_iota(jnp.int32, (1, length), 1)
        good = (pos == 0) | ((pos < lengths[home]) & (keys == 1))
        good = jnp.broadcast_to(jnp.where(good, 1.0, 0.0), (8, length)).astype(bf16)
        real = length // self.p.groups
        padded = self.rows // self.p.groups
        row = lax.broadcasted_iota(jnp.int32, (self.rows, length), 0)
        col = lax.broadcasted_iota(jnp.int32, (self.rows, length), 1)
        hit = (col == row // padded * real + row % padded) & (row % padded < real)
        self.valid[...] = nt(jnp.where(hit, 1.0, 0.0).astype(bf16), good)[:, 0:1]
        self.sid = script_ids[home]

    def norm1(self):
        self.emb[...] = jnp.where(self.sid == 1, self.vec(T1), self.vec(T0))

        def body(i):
            at = ds(i * self.step, self.step)
            hat, mean, inv = normalize(self.x[at, :].astype(f32) + self.emb[...])
            self.stats[at, 0:1] = mean
            self.stats[at, 1:2] = inv
            self.h1[at, :] = (hat * self.vec(G1) + self.vec(B1)).astype(bf16)

        loop(self.rows // self.step, body)

    def project(self, i, n=256):
        d = self.d

        def body(k):
            at = ds(k * n, n, 128)
            value = nn(self.h1[...], self.weight(QKV + i, at))
            if i != 1:
                value = value + self.vecs[QB if i == 0 else VB : (QB if i == 0 else VB) + 1, at]
            self.qkv[:, ds(i * d + k * n, n, 128)] = value.astype(bf16)

        loop(d // n, body)

    def half(self, h, value):
        lane = lax.broadcasted_iota(jnp.int32, value.shape, 1)
        return jnp.where(lane // DH == h, value, jnp.zeros_like(value))

    def pick(self, a, b):
        lane = lax.broadcasted_iota(jnp.int32, a.shape, 1)
        return jnp.where(lane < DH, a, b)

    def lanes(self, p):
        return [ds(i * self.d + p * 128, 128, 128) for i in range(3)]

    def probs_out(self, p):
        slot = p % 2
        return pltpu.make_async_copy(self.probs.at[slot], self.kept.at[p], self.out_sem.at[slot])

    def probs_in(self, p):
        slot = p % 2
        return pltpu.make_async_copy(self.kept.at[p], self.probs.at[slot], self.in_sem.at[slot])

    def attend(self, p):
        aq, ak, av = self.lanes(p)
        q = self.qkv[:, aq] * jnp.asarray(DH**-0.5, bf16)
        k, v = self.qkv[:, ak], self.qkv[:, av]
        valid = self.valid[...] > 0

        @pl.when(p >= 2)
        def _():
            self.probs_out(p - 2).wait()

        contexts = []
        for h in range(2):
            s = nt(k, self.half(h, q))
            s = jnp.where(valid, s, -1e9)
            e = jnp.exp(s - jnp.max(s, axis=0, keepdims=True))
            probs = (e * (1.0 / total(e))).astype(bf16)
            self.probs[p % 2, h] = probs
            contexts.append(tn(probs, v))
        self.ctx[:, ds(p * 128, 128, 128)] = self.pick(*contexts).astype(bf16)
        self.probs_out(p).start()

    def mid_norm(self, n=256):
        def body(k):
            at = ds(k * n, n, 128)
            self.mid[:, at] = nn(self.ctx[...], self.weight(OUT, at))

        loop(self.d // n, body)

        def norm(i):
            at = ds(i * self.step, self.step)
            v = self.x[at, :].astype(f32) + self.emb[...] + (self.mid[at, :] + self.vec(OB))
            self.mid[at, :] = v
            hat, mean, inv = normalize(v)
            self.stats[at, 2:3] = mean
            self.stats[at, 3:4] = inv
            self.h2[at, :] = (hat * self.vec(G2) + self.vec(B2)).astype(bf16)

        loop(self.rows // self.step, norm)

    def mlp_up(self, j, n=256):
        def body(k):
            at = ds(j * self.d + k * n, n, 128)
            pre = nn(self.h2[...], self.weight(UP + j, ds(k * n, n, 128))) + self.b_up[:, at]
            cum = 0.5 * (1.0 + lax.erf(pre * 2.0**-0.5))
            den = jnp.exp(-0.5 * pre * pre) * (2.0 * jnp.pi) ** -0.5
            self.act[:, at] = (pre * cum).astype(bf16)
            self.slope[:, at] = (cum + pre * den).astype(bf16)

        loop(self.d // n, body)

    def down(self, b):
        return self.w_down.at[b // 4, (b // 2) % 2, b % 2]

    def dw_down(self, b):
        u = self.hidden // 8
        grad = tn(self.act[:, ds(b * u, u, 128)], self.cot[...])
        self.p_down[0, b // 4, (b // 2) % 2, b % 2] = grad.astype(bf16)

    def grad_pre(self, b):
        u = self.hidden // 8
        at = ds(b * u, u, 128)
        g = (nt(self.cot[...], self.down(b)[...]) * self.slope[:, at].astype(f32)).astype(bf16)
        self.slope[:, at] = g
        self.up_sums[:, at] = total(g.astype(f32))

    def mlp_down(self, n=256):
        def body(k):
            at = ds(k * n, n, 128)
            w = self.w_down[:, :, :, :, at].reshape(self.hidden, n)
            value = self.mid[:, at] + (nn(self.act[...], w) + self.vecs[DB : DB + 1, at])
            self.out[:, at] = value.astype(bf16)

        loop(self.d // n, body)

    def grad_h2(self, j):
        m = self.rows // 2

        def body(i):
            at = ds(i * m, m)
            value = nt(self.slope[at, ds(j * self.d, self.d, 128)], self.weight(UP + j))
            if j == 0:
                self.wide[at, :] = value
            else:
                self.wide[at, :] += value

        loop(2, body)

    def dw_up(self, j, n=256):
        def body(k):
            grad = tn(self.h2[...], self.slope[:, ds(j * self.d + k * n, n, 128)])
            self.w[UP + j, :, :, :, :, ds(k * n, n, 128)] = self.eighths(grad).astype(bf16)

        loop(self.d // n, body)

    def back2(self):
        zero = jnp.zeros((1, self.d), f32)

        def body(i, sums):
            at = ds(i * self.step, self.step)
            inv = self.stats[at, 3:4]
            hat = (self.mid[at, :] - self.stats[at, 2:3]) * inv
            g = self.wide[at, :]
            cot = self.cot[at, :].astype(f32)
            value = cot + norm_backward(g, hat, inv, self.vec(G2))
            self.mid[at, :] = value
            low = value.astype(bf16)
            self.gb[at, :] = low
            terms = (g * hat, g, cot, low.astype(f32))
            return tuple(s + total(t) for s, t in zip(sums, terms))

        sums = lax.fori_loop(0, self.rows // self.step, body, (zero,) * 4)
        for row, s in zip((G2, B2, DB, OB), sums):
            self.sums[row : row + 1, :] = s

    def grad_ctx(self):
        m = self.rows // 2

        def body(i):
            at = ds(i * m, m)
            self.gctx[at, :] = nt(self.gb[at, :], self.weight(OUT)).astype(bf16)

        loop(2, body)

    def dw_out(self, n=256):
        def body(k):
            at = ds(k * n, n, 128)
            grad = tn(self.ctx[...], self.gb[:, at])
            self.w[OUT, :, :, :, :, at] = self.eighths(grad).astype(bf16)

        loop(self.d // n, body)

    def attend_back(self, p, last):
        aq, ak, av = self.lanes(p)
        q, k, v = self.qkv[:, aq], self.qkv[:, ak], self.qkv[:, av]
        g = self.gctx[:, aq]

        @pl.when(p + 1 < last)
        def _():
            self.probs_in(p + 1).start()

        self.probs_in(p).wait()
        dq, dk, dv = [], [], []
        for h in range(2):
            probs = self.probs[p % 2, h]
            dv.append(nn(probs, g))
            grad = nt(v, self.half(h, g))
            wide = probs.astype(f32)
            grad = (wide * (grad - total(wide * grad))).astype(bf16)
            dk.append(nn(grad, q))
            dq.append(tn(grad, k))
        dq = (self.pick(*dq) * DH**-0.5).astype(bf16)
        dv = self.pick(*dv).astype(bf16)
        self.qkv[:, aq] = dq
        self.qkv[:, ak] = (self.pick(*dk) * DH**-0.5).astype(bf16)
        self.qkv[:, av] = dv
        self.sums[QB : QB + 1, aq] = total(dq.astype(f32))
        self.sums[VB : VB + 1, aq] = total(dv.astype(f32))

    def grad_h1(self, g, n=256):
        m = self.rows // 2

        def body(i):
            at = ds(i * m, m)
            value = None
            for k in range(3):
                w = self.weight(QKV + k, pl.ds(g * n, n))
                term = nt(self.qkv[at, pl.ds(k * self.d + g * n, n)], w)
                value = term if value is None else value + term
            if g == 0:
                self.wide[at, :] = value
            else:
                self.wide[at, :] += value

        loop(2, body)

    def dw_qkv(self, g, n=256):
        for k in range(3):
            grad = tn(self.h1[...], self.qkv[:, pl.ds(k * self.d + g * n, n)])
            self.w[QKV + k, :, :, :, :, pl.ds(g * n, n)] = self.eighths(grad).astype(bf16)

    def back1(self):
        zero = jnp.zeros((1, self.d), f32)

        def body(i, sums):
            at = ds(i * self.step, self.step)
            inv = self.stats[at, 1:2]
            hat = (self.x[at, :].astype(f32) + self.emb[...] - self.stats[at, 0:1]) * inv
            g = self.wide[at, :]
            value = self.mid[at, :] + norm_backward(g, hat, inv, self.vec(G1))
            self.gx[at, :] = value.astype(bf16)
            return tuple(s + total(t) for s, t in zip(sums, (g * hat, g, value)))

        sums = lax.fori_loop(0, self.rows // self.step, body, (zero,) * 3)
        self.sums[G1 : G1 + 1, :] = sums[0]
        self.sums[B1 : B1 + 1, :] = sums[1]
        self.sums[T0 : T0 + 1, :] = jnp.where(self.sid == 1, 0.0, sums[2])
        self.sums[T1 : T1 + 1, :] = jnp.where(self.sid == 1, sums[2], 0.0)


def kernel(outer, groups, names, *refs):
    r = dict(zip(names, refs, strict=True))
    p = Place(outer, groups)
    L = Layer(p, r)
    d, hidden = L.d, L.hidden
    nh = hidden // d
    real = r["patches"].shape[1]
    strips = r["patches"].shape[0]
    per = d // (8 * groups)
    u = d // 8
    n_down = d // 256
    w, w_down, stage = r["w"], r["w_down"], r["stage"]

    gs = []

    def add(shard, block, part, land, settle=None):
        gs.append(
            Gather(p, len(gs), shard, block, part, land, r["g_send"], r["g_recv"], settle)
        )

    add(
        r["s_small"],
        lambda y, x, c: r["small"].at[y * 4 + x * 2 + c],
        lambda ref, h: ref.at[pl.ds(h * (groups // 2), groups // 2)],
        lambda z: r["small"].at[p.y * 4 + p.x * 2 + p.c, z],
    )

    def add_square(i, shard):
        def settle(block):
            block[...] = stage[i].astype(f32).reshape(u, d).astype(bf16)

        add(
            shard,
            lambda y, x, c: w.at[i, y, x, c],
            lambda ref, h: ref.at[pl.ds(h * (u // 2), u // 2)],
            lambda z: stage.at[i, z],
            settle,
        )

    for i in range(3):
        add_square(QKV + i, r["s_qkv"].at[:, pl.ds(i * d, d)])
    add_square(OUT, r["s_out"])
    for i in range(nh):
        add_square(UP + i, r["s_up"].at[:, pl.ds(i * d, d)])
    hu = hidden // 8
    hr = hu // groups
    for i in range(n_down):
        cols = pl.ds(i * 256, 256)
        add(
            r["s_down"].at[:, cols],
            lambda y, x, c, cols=cols: w_down.at[y, x, c, :, cols],
            lambda ref, h: ref.at[pl.ds(h * (hu // 2), hu // 2)],
            lambda z, cols=cols: w_down.at[p.y, p.x, p.c, ds(z * hr, hr), cols],
        )
    xs = Rows(p, r["xp"], r["x"], r["x_send"], r["x_recv"])
    cs = Rows(p, r["cp"], r["cot"], r["c_send"], r["c_recv"])
    last = len(gs)

    def gather_tick(t):
        for lag, act in enumerate(("z_start", "z_finish", "mid", "diag", "finish")):
            if 0 <= t - lag < last:
                getattr(gs[t - lag], act)()

    ss = []

    def give(part, bufs, out):
        ss.append(Scatter(p, len(ss), part, bufs, out, r["s_send"], r["s_recv"]))

    def bufs(kind, i):
        flat = kind == "flat"
        found = [r[f"{kind}_{name}"].at[i] for name in ("core", "r1", "r2", "q1", "q2")]
        slot = stage.at[pl.ds(UP + i if i < nh else OUT, 1)] if flat else r[f"{kind}_zs"].at[i]
        return found + [slot, r[f"{kind}_zr"].at[i]]

    for i in range(n_down):
        cols = pl.ds(i * 256, 256)
        give(r["p_down"].at[:, :, :, :, :, cols], bufs("tall", i), [r["o_down"].at[:, cols]])
    for i in range(nh):
        give(w.at[pl.ds(UP + i, 1)], bufs("flat", i), [r["o_up"].at[:, pl.ds(i * d, d)]])
    give(w.at[pl.ds(OUT, 1)], bufs("flat", nh), [r["o_out"]])
    for g in range(d // 256):
        cols = pl.ds(g * 256, 256)
        outs = [r["o_qkv"].at[:, pl.ds(k * d + g * 256, 256)] for k in range(3)]
        give(w.at[pl.ds(QKV, 3), :, :, :, :, cols], bufs("head", g), outs)

    def scatter_tick(t):
        for lag, act in enumerate(("core_add", "pass_on", "z_start", "finish")):
            if 0 <= t - lag < len(ss):
                getattr(ss[t - lag], act)()

    ys = Rows(p, r["xp"], r["out"], r["y_send"], r["y_recv"])
    ds_ = Rows(p, r["cp"], L.gx, r["d_send"], r["d_recv"])
    ts = Tally(p, r["value"], r["got"], r["t_send"], r["t_recv"])

    p.greet()
    gather_tick(0)
    gather_tick(1)
    for src, dst in ((r["patches"], r["xp"]), (r["cotangent"], r["cp"])):
        dst[...] = jnp.zeros_like(dst)
        for s in range(strips):
            dst[s, :real] = src[s]
    gather_tick(2)
    xs.in_start()
    L.mask(r["lengths"], r["script_ids"], r["key_mask"])
    gather_tick(3)
    gather_tick(4)
    L.vectors()
    xs.in_finish()
    L.norm1()
    gather_tick(5)
    L.project(0)
    gather_tick(6)
    cs.in_start()
    L.project(1)
    gather_tick(7)
    L.project(2)
    gather_tick(8)
    pairs = d // 128

    def attend(i):
        L.attend(i)
        for k, t in ((1, 9), (3, 10)):

            @pl.when(i == k)
            def _():
                gather_tick(t)

    loop(pairs, attend)
    for i in (pairs - 2, pairs - 1):
        L.probs_out(i).wait()
    L.mid_norm()
    gather_tick(11)
    for j in range(nh - 1):
        L.mlp_up(j)
    gather_tick(12)
    L.mlp_up(nh - 1)
    cs.in_finish()
    xs.in_sent()
    cs.in_sent()

    def down(i):
        L.dw_down(i)

        @pl.when(i == 3)
        def _():
            gather_tick(13)

    loop(8, down)
    for i in range(n_down):
        ss[i].start()
    for t in range(14, last + 4):
        gather_tick(t)
    scatter_tick(0)

    def grad_pre(i):
        L.grad_pre(i)

        @pl.when(i == 3)
        def _():
            scatter_tick(1)

    loop(8, grad_pre)
    scatter_tick(2)
    for j in range(nh):
        L.grad_h2(j)
    for j in range(nh):
        L.dw_up(j)
        ss[n_down + j].start()
        scatter_tick(n_down + j)
    L.mlp_down()
    ys.out_start()
    L.back2()
    L.grad_ctx()
    L.dw_out()
    at = n_down + nh
    ss[at].start()
    scatter_tick(at)
    L.probs_in(0).start()
    for g in range(d // 256):
        loop(2, lambda i: L.attend_back(2 * g + i, pairs))
        L.grad_h1(g)
        L.dw_qkv(g)
        at += 1
        ss[at].start()
        if g < d // 256 - 1:
            scatter_tick(at)
    L.back1()
    ds_.out_start()
    r["value"][0] = jnp.concatenate(
        [r["sums"][0:10, :]]
        + [L.up_sums[:, j * d : (j + 1) * d] for j in range(nh)]
        + [jnp.zeros((6 - nh, d), f32)]
    )
    ts.start()
    scatter_tick(at)
    ts.step(0)
    scatter_tick(at + 1)
    ts.step(1)
    scatter_tick(at + 2)
    ts.step(2)
    ys.out_finish()
    for s in range(strips):
        r["o_out_rows"][s] = r["xp"][s, :real]
    r["o_tally"][...] = ts.finish()
    scatter_tick(at + 3)
    ds_.out_finish()
    for s in range(strips):
        r["o_grad_rows"][s] = r["cp"][s, :real]
    for s in ss:
        s.drain()


def on_device(outer, groups, *args):
    (patches, cotangent, lengths, script_ids, key_mask, norm1_gain, norm1_bias, w_qkv, q_bias,
     v_bias, w_attn_out, attn_out_bias, norm2_gain, norm2_bias, w_up, up_bias, w_down, down_bias,
     script_table) = args
    strips, part_rows, d = patches.shape
    hidden = w_up.shape[1]
    parts = 8 * groups
    pad_rows = round_up(part_rows, 16)
    rows = groups * pad_rows
    vectors = [norm1_gain, norm1_bias, q_bias, v_bias, attn_out_bias, norm2_gain, norm2_bias,
               down_bias, script_table[0], script_table[1]]
    weights = [w_qkv, w_attn_out, w_up, w_down]
    if outer > 1:
        mates = [[g * outer + i for i in range(outer)] for g in range(8)]
        seq = lax.axis_index("seq")

        def widen(a):
            a = lax.all_gather(a, ("seq",), axis=0, tiled=True)
            a = lax.all_gather(a, "dp", axis=0, tiled=True, axis_index_groups=mates)
            n = a.shape[0] // groups
            return lax.dynamic_slice_in_dim(a, seq * n, n, axis=0)

        vectors = [widen(a) for a in vectors]
        up_bias = widen(up_bias)
        weights = [widen(a) for a in weights]
    c = vectors[0].shape[0]
    small = jnp.concatenate(
        [
            jnp.pad(jnp.stack(vectors), ((0, 0), (0, 128 - c))),
            jnp.pad(up_bias[None], ((0, 5), (0, 128 - up_bias.shape[0]))),
        ]
    )
    vm = pl.BlockSpec(memory_space=pltpu.VMEM)
    sm = pl.BlockSpec(memory_space=pltpu.SMEM)
    anywhere = pl.BlockSpec(memory_space=pl.ANY)
    sems = pltpu.SemaphoreType.DMA
    nh = hidden // d
    u, r, nd, ng = d // 8, d // parts, d // 256, d // 256
    ins = ["s_small", "s_qkv", "s_out", "s_up", "s_down", "patches", "cotangent", "key_mask",
           "lengths", "script_ids"]
    outs = {
        "o_qkv": ((r, 3 * d), f32),
        "o_out": ((r, d), f32),
        "o_up": ((r, hidden), f32),
        "o_down": ((hidden // parts, d), f32),
        "o_tally": ((16, d), f32),
        "o_out_rows": (patches.shape, bf16),
        "o_grad_rows": (patches.shape, bf16),
        "kept": ((d // 128, 2, rows, rows), bf16),
    }
    scratch = {
        "small": ((8, groups, 16, 128), bf16),
        "stage": ((4 + nh, groups, r, d), bf16),
        "w": ((4 + nh, 2, 2, 2, u, d), bf16),
        "w_down": ((2, 2, 2, hidden // 8, d), bf16),
        "p_down": ((1, 2, 2, 2, hidden // 8, d), bf16),
        "xp": ((strips, pad_rows, d), bf16),
        "cp": ((strips, pad_rows, d), bf16),
        "x": ((rows, d), bf16),
        "cot": ((rows, d), bf16),
        "valid": ((rows, 1), f32),
        "vecs": ((16, d), f32),
        "b_up": ((1, hidden), f32),
        "up_sums": ((1, hidden), f32),
        "sums": ((16, d), f32),
        "emb": ((1, d), f32),
        "stats": ((rows, 4), f32),
        "h1": ((rows, d), bf16),
        "qkv": ((rows, 3 * d), bf16),
        "probs": ((2, 2, rows, rows), bf16),
        "ctx": ((rows, d), bf16),
        "mid": ((rows, d), f32),
        "wide": ((rows, d), f32),
        "h2": ((rows, d), bf16),
        "act": ((rows, hidden), bf16),
        "slope": ((rows, hidden), bf16),
        "value": ((4, 16, d), f32),
        "got": ((2 + groups, 16, d), f32),
    }
    for kind, count, k, uu, n in (
        ("tall", nd, 1, hidden // 8, 256),
        ("flat", nh + 1, 1, u, d),
        ("head", ng, 3, u, 256),
    ):
        rr = uu // groups
        scratch[f"{kind}_core"] = ((count, k, 2, 2, uu, n), bf16)
        scratch[f"{kind}_r1"] = ((count, k, 2, uu // 2, n), bf16)
        scratch[f"{kind}_r2"] = ((count, k, 2, uu // 2, n), bf16)
        scratch[f"{kind}_q1"] = ((count, k, uu // 2, n), bf16)
        scratch[f"{kind}_q2"] = ((count, k, uu // 2, n), bf16)
        if kind != "flat":
            scratch[f"{kind}_zs"] = ((count, k, groups, rr, n), bf16)
        scratch[f"{kind}_zr"] = ((count, groups - 1, k, rr, n), bf16)
    n_gather = 5 + nh + nd
    n_scatter = nd + nh + 1 + ng
    semaphores = {
        "g_send": (n_gather, WIRE), "g_recv": (n_gather, WIRE),
        "s_send": (n_scatter, HOPS), "s_recv": (n_scatter, HOPS),
        "t_send": (2 + groups,), "t_recv": (2 + groups,),
        "out_sem": (2,), "in_sem": (2,),
    }
    for name in "xcyd":
        semaphores[f"{name}_send"] = (groups - 1,)
        semaphores[f"{name}_recv"] = (groups - 1,)
    names = ins + list(outs) + list(scratch) + list(semaphores)

    def body(*refs):
        refs = dict(zip(names, refs, strict=True))
        act = refs["act"]
        refs["out"] = refs["h2"]
        refs["gb"] = act.at[:, pl.ds(0, d)]
        refs["gctx"] = act.at[:, pl.ds(d, d)]
        refs["gx"] = act.at[:, pl.ds(2 * d, d)]
        kernel(outer, groups, list(refs), *refs.values())

    res = pl.pallas_call(
        body,
        out_shape=[jax.ShapeDtypeStruct(*s) for s in outs.values()],
        in_specs=[vm] * 8 + [sm] * 2,
        out_specs=[vm] * 7 + [anywhere],
        scratch_shapes=[pltpu.VMEM(*s) for s in scratch.values()]
        + [sems(s) for s in semaphores.values()],
        compiler_params=pltpu.CompilerParams(
            collective_id=0, has_side_effects=True, vmem_limit_bytes=63 * 2**20
        ),
    )(small, *weights, patches, cotangent, key_mask, lengths, script_ids)
    shards = list(res[:4])
    tally = res[4]
    if outer > 1:

        def narrow(a):
            a = lax.psum(a, "dp", axis_index_groups=mates)
            a = lax.all_gather(a, ("seq",), axis=0, tiled=True)
            at = (lax.axis_index("dp") % outer) * groups + lax.axis_index("seq")
            n = a.shape[0] // groups // outer
            return lax.dynamic_slice_in_dim(a, at * n, n, axis=0)

        shards = [narrow(a) for a in shards]
        tally = lax.psum(tally, "dp", axis_index_groups=mates)
    me = lax.axis_index("dp") * groups + lax.axis_index("seq")
    n = d // (parts * outer)
    vec = lax.dynamic_slice_in_dim(tally[:10], me * n, n, axis=1)
    m = hidden // (parts * outer)
    vup = lax.dynamic_slice_in_dim(tally[10 : 10 + nh].reshape(hidden), me * m, m, axis=0)
    return (
        res[5], res[6], vec[G1], vec[B1], shards[0], vec[QB], vec[VB], shards[1], vec[OB], vec[G2],
        vec[B2], shards[2], vup, shards[3], vec[DB], vec[T0 : T1 + 1],
    )


def solution(mesh):
    dp, seq = mesh.shape["dp"], mesh.shape["seq"]
    both = ("dp", "seq")
    one, two = P(both), P(both, None)
    rows = P("dp", "seq", None)
    return jax.shard_map(
        functools.partial(on_device, dp // 8, seq),
        mesh=mesh,
        in_specs=(
            rows, rows, P("dp"), P("dp"), P("dp", None), one, one, two, one, one, two, one, one,
            one, two, one, two, one, P(None, both),
        ),
        out_specs=(
            rows, rows, one, one, two, one, one, two, one, one, one, two, one, two, one,
            P(None, both),
        ),
        check_vma=False,
    )
```

profile of v0, /device:TPU:0, one launch (start us, length us, event | category | flops | bytes accessed | tf_op | source)
XLA Modules:
  0.0 236.6 jit_solution(7530558054024401972)
XLA Ops:
  0.7 1.5 stack.36
  2.1 1.3 fusion.2.refs_0_
  3.4 218.5 %shard_map.306 = (f32[24,2304]{1,0:T(8,128)}, f32[24,768]{1,0:T(8,128)}, f32[24,3072]{1,0:T(8,128)}, f32[96,768]{1,0:T(8,128)}, f32[16,768]{1,0:T(8,128)}, /*ind...) custom-call(bf16[16,128]{1,0:T(8,128)(2,1)} %fusion.2.refs_0_, ...), custom_call_target="tpu_custom_call" | custom-call | tf_op jit(solution)/shard_map/pallas_call | solution.py:1019
  221.9 1.6 dynamic-slice_bitcast_fusion
  223.5 0.7 slice.44
  224.3 0.6 dynamic_slice.7
  224.9 1.3 dynamic-slice.8
  226.2 1.9 copy.41
  228.1 1.9 copy.42
  230.1 1.6 copy.43
  231.7 1.5 copy.44
  233.2 1.7 copy.45
  234.9 1.7 copy.46
  (1 shorter events, 0.0 us)
where the time goes:
time: 238 us; the launch traced here: 237 us
  Pallas kernels  219 us (92%)
  local copies, waits for them, and re-layouts  16.2 us (7%)
    pallas_call x1, Pallas kernels, on_device(): pl.pallas_call(body, out_shape=[jax.ShapeDtypeStruct(*s) for s in outs.va...  219 us
    unnamed x6, local copies, waits for them, and re-layouts  10.4 us

commit v1 on v0

--- a/solution.py
+++ b/solution.py
@@ -12,8 +12,10 @@
 f32 = jnp.float32
 bf16 = jnp.bfloat16
 epsilon = 1e-06
-WIRE = 12
-HOPS = 8
+WIRE = 13
+FAR = 12
+DIRECT = 1
+HOPS = 9
 QKV, OUT, UP = 0, 3, 4
 G1, B1, QB, VB, OB, G2, B2, DB, T0, T1 = range(10)
 
@@ -56,15 +58,62 @@
     )
 
 
+(ZS, ZE, MX, MY, DX, DY, FIN, ST, CA, PX, PY, ZT, FI, ROW, IN, OUT_, ZF, ZP) = range(18)
+(SMALL, WQ, WK, WV, WO, WU, WD, GD, GU, GO, GQ, X_IN, C_IN, Y_OUT, R_OUT) = range(1, 16)
+(PREP, MASK, VEC, NORM1, PROJ, ATT, MID, UP_, DWDOWN, GPRE, DOWN, GU_, BACK2, GCTX, DWUP, ATTB,
+ GQ_, DWQKV, BACK1, DWOUT, SENT, SENTX, T) = range(100, 123)
+SCHEDULE = (
+    (ZS, SMALL, 0), (ZS, WQ, 0), (ZS, WK, 0), (PREP, 0, 0), (ZS, WV, 0), (MASK, 0, 0),
+    (ZS, WO, 0), (ZE, SMALL, 0), (ZF, WQ, 0), (ROW, X_IN, 0), (MX, SMALL, 0), (MY, SMALL, 0),
+    (ZF, WK, 0), (DX, SMALL, 0), (DY, SMALL, 0), (ZF, WV, 0), (FIN, SMALL, 0), (VEC, 0, 0),
+    (ZF, WO, 0), (ZE, WQ, 0), (ZS, WU, 0), (ROW, X_IN, 1), (ZE, WK, 0), (ZE, WV, 0), (MX, WQ, 0),
+    (MY, WQ, 0), (ZE, WO, 0), (ZS, WU, 1), (ZF, WU, 0), (ROW, X_IN, 2), (MX, WK, 0), (MY, WK, 0),
+    (MX, WV, 0), (ZS, WU, 2), (MY, WV, 0), (ZF, WU, 1), (ZE, WU, 0), (DX, WQ, 0), (DY, WQ, 0),
+    (ZS, WU, 3), (ZS, WD, 0), (MX, WO, 0), (MY, WO, 0), (IN, X_IN, 0), (NORM1, 0, 0),
+    (ROW, C_IN, 0), (DX, WK, 0), (DY, WK, 0), (FIN, WQ, 0), (PROJ, 0, 0), (DX, WV, 0),
+    (DY, WV, 0), (ZE, WU, 1), (ZF, WU, 2), (FIN, WK, 0), (PROJ, 0, 1), (ZF, WU, 3), (FIN, WV, 0),
+    (PROJ, 0, 2), (MX, WU, 0), (MY, WU, 0), (ATT, 0, 0), (ZS, WD, 1), (DX, WO, 0), (DY, WO, 0),
+    (ZF, WD, 0), (ATT, 0, 1), (ROW, C_IN, 1), (MX, WU, 1), (MY, WU, 1), (ATT, 0, 2), (DX, WU, 0),
+    (DY, WU, 0), (ZE, WU, 2), (ZE, WU, 3), (ATT, 0, 3), (ZS, WD, 2), (DX, WU, 1), (DY, WU, 1),
+    (ZF, WD, 1), (ATT, 0, 4), (ZE, WD, 0), (ATT, 0, 5), (SENTX, 0, 0), (ROW, C_IN, 2),
+    (MX, WU, 2), (MY, WU, 2), (FIN, WO, 0), (MID, 0, 0), (MX, WU, 3), (MY, WU, 3), (FIN, WU, 0),
+    (UP_, 0, 0), (ZE, WD, 1), (ZF, WD, 2), (FIN, WU, 1), (UP_, 0, 1), (MX, WD, 0), (MY, WD, 0),
+    (DX, WU, 2), (DY, WU, 2), (FIN, WU, 2), (UP_, 0, 2), (DX, WU, 3), (DY, WU, 3), (ZE, WD, 2),
+    (FIN, WU, 3), (UP_, 0, 3), (IN, C_IN, 0), (DWDOWN, 0, 0), (MX, WD, 1), (MY, WD, 1),
+    (DWDOWN, 0, 1), (DWDOWN, 0, 2), (DWDOWN, 0, 3), (DX, WD, 0), (DY, WD, 0), (DWDOWN, 0, 4),
+    (DWDOWN, 0, 5), (DWDOWN, 0, 6), (DWDOWN, 0, 7), (ST, GD, 0), (ST, GD, 1), (ST, GD, 2),
+    (MX, WD, 2), (MY, WD, 2), (CA, GD, 0), (DX, WD, 1), (DY, WD, 1), (CA, GD, 1), (DX, WD, 2),
+    (DY, WD, 2), (CA, GD, 2), (FIN, WD, 0), (FIN, WD, 1), (FIN, WD, 2), (GPRE, 0, 0),
+    (GPRE, 0, 1), (GPRE, 0, 2), (GPRE, 0, 3), (PX, GD, 0), (PY, GD, 0), (GPRE, 0, 4),
+    (GPRE, 0, 5), (GPRE, 0, 6), (GPRE, 0, 7), (DOWN, 0, 0), (OUT_, Y_OUT, 0), (PX, GD, 1),
+    (PY, GD, 1), (GU_, 0, 0), (GU_, 0, 1), (PY, GD, 2), (PX, GD, 2), (GU_, 0, 2), (GU_, 0, 3),
+    (SENT, 0, 0), (DWUP, 0, 0), (ST, GU, 0), (ZT, GD, 0), (DWUP, 0, 1), (ST, GU, 1), (ZT, GD, 1),
+    (CA, GU, 0), (DWUP, 0, 2), (ST, GU, 2), (ZT, GD, 2), (CA, GU, 1), (DWUP, 0, 3), (ST, GU, 3),
+    (CA, GU, 2), (BACK2, 0, 0), (PX, GU, 0), (PY, GU, 0), (CA, GU, 3), (GCTX, 0, 0), (ATTB, 0, 0),
+    (PX, GU, 1), (PY, GU, 1), (ATTB, 0, 1), (ZP, GD, 0), (GQ_, 0, 0), (PX, GU, 2), (PY, GU, 2),
+    (DWQKV, 0, 0), (ST, GQ, 0), (ZP, GD, 1), (ZT, GU, 0), (ZP, GD, 2), (ATTB, 0, 2), (FI, GD, 0),
+    (PX, GU, 3), (PY, GU, 3), (CA, GQ, 0), (ATTB, 0, 3), (FI, GD, 1), (ZT, GU, 1), (GQ_, 0, 1),
+    (ZP, GU, 0), (ZT, GU, 2), (DWQKV, 0, 1), (ST, GQ, 1), (FI, GD, 2), (ZT, GU, 3), (ATTB, 0, 4),
+    (ZP, GU, 1), (FI, GU, 0), (PX, GQ, 0), (PY, GQ, 0), (CA, GQ, 1), (ATTB, 0, 5), (ZP, GU, 2),
+    (ZP, GU, 3), (GQ_, 0, 2), (BACK1, 0, 0), (OUT_, R_OUT, 0), (FI, GU, 1), (ZT, GQ, 0), (T, 0, 0),
+    (DWQKV, 0, 2), (ST, GQ, 2), (FI, GU, 2), (DWOUT, 0, 0), (ST, GO, 0), (T, 0, 1), (FI, GU, 3),
+    (PX, GQ, 1), (PY, GQ, 1), (CA, GQ, 2), (CA, GO, 0), (ZT, GQ, 1), (PY, GQ, 2), (T, 0, 2),
+    (PX, GQ, 2), (PY, GO, 0), (PX, GO, 0), (ZT, GQ, 2), (ZT, GO, 0), (ZP, GQ, 0), (ZP, GQ, 1),
+    (ZP, GQ, 2), (ZP, GO, 0), (FI, GQ, 0), (FI, GQ, 1), (FI, GQ, 2), (FI, GO, 0),
+)
+
+
 class Place:
     def __init__(self, outer, groups):
         self.dp = lax.axis_index("dp")
         self.z = lax.axis_index("seq")
+        assert groups == 4
         self.groups = groups
         b = self.dp // outer
         self.c = b % 2
         self.x = (b // 2) % 2
         self.y = b // 4
+        self.inner = (self.z == 1) | (self.z == 2)
         self.to_c = (self.dp + outer * (1 - 2 * self.c), self.z)
         self.to_x = (self.dp + outer * (2 - 4 * self.x), self.z)
         self.to_y = (self.dp + outer * (4 - 8 * self.y), self.z)
@@ -96,17 +145,44 @@
     def copy(self, k, ref, to):
         return remote(ref, ref, self.send.at[self.i, k], self.recv.at[self.i, k], to)
 
-    def z_copy(self, j, owner):
+    def z_wire(self, k):
+        p, z = self.p, self.p.z
+        if k < 3:
+            src, owner, to = self.shard, z, ((z + 1) % 4, (z + 2) % 4, (z + 3) % 4)[k]
+        elif self.i < DIRECT:
+            src, owner, to = self.shard, z, 3 - z
+        else:
+            owner = (z + 2) % 4
+            src, to = self.land(owner), (z + 1) % 4 * (z // 2)
         return remote(
-            self.shard, self.land(owner), self.send.at[self.i, j - 1], self.recv.at[self.i, j - 1],
-            self.p.to_z(self.p.ahead(j)),
+            src, self.land(owner), self.send.at[self.i, k], self.recv.at[self.i, k], p.to_z(to)
         )
 
+    def z_got(self, k):
+        z = self.p.z
+        owner = ((z + 3) % 4, (z + 2) % 4, (z + 1) % 4)[k] if k < 3 else 3 - z
+        ref = self.land(owner)
+        remote(
+            ref, ref, self.send.at[self.i, k], self.recv.at[self.i, k], self.p.to_z((z + 1) % 4)
+        ).wait_recv()
+
     def z_start(self):
         p = self.p
-        for j in range(1, p.groups):
-            self.z_copy(j, p.z).start()
+        pl.when(p.z < 3)(lambda: self.z_wire(0).start())
+        self.z_wire(1).start()
+        pl.when(p.z > 0)(lambda: self.z_wire(2).start())
+        if self.i < DIRECT:
+            pl.when(jnp.logical_not(p.inner))(lambda: self.z_wire(FAR).start())
         self.land(p.z)[...] = self.shard[...]
+
+    def z_far(self):
+        if self.i < DIRECT:
+            return
+
+        @pl.when(self.p.inner)
+        def _():
+            self.z_got(1)
+            self.z_wire(FAR).start()
 
     def xy(self, k):
         p = self.p
@@ -131,36 +207,41 @@
             return self.copy(9, by(), p.to_c)
         return self.copy(k, self.part(bd(), k - 10), p.to_c)
 
-    def z_finish(self):
-        p = self.p
-        for j in range(1, p.groups):
-            self.z_copy(j, p.behind(j)).wait_recv()
+    def z_end(self):
+        p = self.p
+        pl.when(p.z > 0)(lambda: self.z_got(0))
+        pl.when(p.z < 3)(lambda: self.z_got(2))
+
+        @pl.when(jnp.logical_not(p.inner))
+        def _():
+            self.z_got(1)
+            self.z_got(FAR)
+
+        if self.i < DIRECT:
+            pl.when(p.inner)(lambda: self.z_got(1))
         if self.settle is not None:
             self.settle(self.block(p.y, p.x, p.c))
         for k in (3, 4, 7):
             self.xy(k).start()
 
-    def mid(self):
-        self.xy(3).wait_recv()
-        self.xy(6).start()
-        self.xy(8).start()
-        self.xy(4).wait_recv()
-        self.xy(5).start()
-        self.xy(9).start()
-
-    def diag(self):
-        self.xy(6).wait_recv()
-        self.xy(10).start()
-        self.xy(5).wait_recv()
-        self.xy(11).start()
+    def pass_on(self, came, on, core):
+        self.xy(came).wait_recv()
+        for k in (on, core):
+            if k is not None:
+                self.xy(k).start()
 
     def finish(self):
-        p = self.p
         for k in (7, 8, 9, 10, 11):
             self.xy(k).wait_recv()
-        for j in range(1, p.groups):
-            self.z_copy(j, p.z).wait_send()
-        for k in range(3, WIRE):
+
+    def sent(self):
+        p = self.p
+        pl.when(p.z < 3)(lambda: self.z_wire(0).wait_send())
+        self.z_wire(1).wait_send()
+        pl.when(p.z > 0)(lambda: self.z_wire(2).wait_send())
+        far = jnp.logical_not(p.inner) if self.i < DIRECT else p.inner
+        pl.when(far)(lambda: self.z_wire(FAR).wait_send())
+        for k in range(3, FAR):
             self.xy(k).wait_send()
 
 
@@ -168,6 +249,7 @@
     def __init__(self, place, parts, strip, send, recv):
         self.p, self.parts, self.strip, self.send, self.recv = place, parts, strip, send, recv
         self.strips, self.rows = parts.shape[0], parts.shape[1]
+        self.pieces = parts.shape[2] // 256
         self.home = place.z - place.c
         self.is_home = (self.home >= 0) & (self.home < self.strips)
 
@@ -177,20 +259,24 @@
     def at(self, z):
         return self.strip.at[ds(z * self.rows, self.rows)]
 
-    def inward(self, j, owner, s):
+    def inward(self, k, j, owner, s):
+        cols = pl.ds(k * 256, 256)
         return remote(
-            self.parts.at[s], self.at(owner), self.send.at[j - 1], self.recv.at[j - 1],
-            self.p.to_z(self.p.ahead(j)),
+            self.parts.at[s, :, cols], self.strip.at[ds(owner * self.rows, self.rows), cols],
+            self.send.at[k, j - 1], self.recv.at[k, j - 1], self.p.to_z(self.p.ahead(j)),
         )
 
-    def in_start(self):
+    def in_start(self, k):
         p = self.p
         for j in range(1, p.groups):
             s = p.ahead(j) - p.c
 
             @pl.when((s >= 0) & (s < self.strips))
             def _():
-                self.inward(j, p.z, self.clip(s)).start()
+                self.inward(k, j, p.z, self.clip(s)).start()
+
+    def in_local(self):
+        p = self.p
 
         @pl.when(self.is_home)
         def _():
@@ -205,8 +291,9 @@
 
         @pl.when(self.is_home)
         def _():
-            for j in range(1, p.groups):
-                self.inward(j, p.behind(j), 0).wait_recv()
+            for k in range(self.pieces):
+                for j in range(1, p.groups):
+                    self.inward(k, j, p.behind(j), 0).wait_recv()
 
     def in_sent(self):
         p = self.p
@@ -215,7 +302,8 @@
 
             @pl.when((s >= 0) & (s < self.strips))
             def _():
-                self.inward(j, p.z, self.clip(s)).wait_send()
+                for k in range(self.pieces):
+                    self.inward(k, j, p.z, self.clip(s)).wait_send()
 
     def outward(self, j, s):
         z = self.p.ahead(j)
@@ -246,17 +334,6 @@
         def _():
             for j in range(1, p.groups):
                 self.outward(j, self.clip(self.home)).wait_send()
-
-
-def add_into(dst, terms, rows, step=48):
-    def body(i):
-        at = ds(i * step, step)
-        value = terms[0][at, :]
-        for term in terms[1:]:
-            value = value + term[at, :]
-        dst[at, :] = value
-
-    loop(rows // step, body)
 
 
 class Scatter:
@@ -280,9 +357,12 @@
             src, dst, to = self.r1.at[:, 1 - p.y], self.q1, p.to_y
         elif k == 4:
             src, dst, to = self.r2.at[:, 1 - p.x], self.q2, p.to_x
+        elif k < 8:
+            z = (p.z + k - 4) % 4
+            src, dst, to = self.zs.at[:, z], self.zr.at[k - 5], p.to_z(z)
         else:
-            z = p.ahead(k - 4)
-            src, dst, to = self.zs.at[:, z], self.zr.at[k - 5], p.to_z(z)
+            z = 1 + p.z // 3
+            src, dst, to = self.zs.at[:, 3 - p.z], self.zr.at[3], p.to_z(z)
         return remote(src, dst, self.send.at[i, k], self.recv.at[i, k], to)
 
     def start(self):
@@ -295,21 +375,24 @@
             for y in range(2):
                 for x in range(2):
                     here = self.core.at[k, y, x]
-                    add_into(here, (here, self.part.at[k, y, x, p.c]), self.u)
+                    here[...] = here[...] + self.part[k, y, x, p.c]
         self.wire(1).start()
         self.wire(2).start()
 
-    def pass_on(self):
+    def pass_x(self):
         p = self.p
         self.wire(1).wait_recv()
         for k in range(self.k):
             here = self.r1.at[k, 1 - p.y]
-            add_into(here, (here, self.core.at[k, 1 - p.y, p.x, self.first]), self.u // 2)
+            here[...] = here[...] + self.core[k, 1 - p.y, p.x, self.first, :]
         self.wire(3).start()
+
+    def pass_y(self):
+        p = self.p
         self.wire(2).wait_recv()
         for k in range(self.k):
             here = self.r2.at[k, 1 - p.x]
-            add_into(here, (here, self.core.at[k, p.y, 1 - p.x, self.second]), self.u // 2)
+            here[...] = here[...] + self.core[k, p.y, 1 - p.x, self.second, :]
         self.wire(4).start()
 
     def z_start(self):
@@ -326,22 +409,44 @@
                 value += mine[...].astype(f32) + got[...].astype(f32)
                 slabs = value.reshape(per, r, self.n)
                 self.zs[k, pl.ds(h * per, per)] = slabs.astype(bf16)
-        for j in range(1, p.groups):
-            self.wire(4 + j).start()
+        pl.when(p.z < 3)(lambda: self.wire(5).start())
+        pl.when(p.z > 0)(lambda: self.wire(7).start())
+
+        @pl.when(jnp.logical_not(p.inner))
+        def _():
+            self.wire(6).start()
+            self.wire(8).start()
+
+    def z_pass(self):
+        @pl.when(self.p.inner)
+        def _():
+            self.wire(8).wait_recv()
+            z = (self.p.z + 2) % 4
+            for k in range(self.k):
+                self.zs[k, z] = self.zs[k, z] + self.zr[3, k]
+            self.wire(6).start()
 
     def finish(self):
         p = self.p
-        for j in range(1, p.groups):
-            self.wire(4 + j).wait_recv()
+        self.wire(6).wait_recv()
         for k in range(self.k):
-            value = self.zs[k, p.z].astype(f32)
-            for j in range(1, p.groups):
-                value += self.zr[j - 1, k].astype(f32)
-            self.out[k][...] = value
+            self.out[k][...] = self.zs[k, p.z].astype(f32) + self.zr[1, k].astype(f32)
+
+        def more(wire, slot):
+            self.wire(wire).wait_recv()
+            for k in range(self.k):
+                self.out[k][...] += self.zr[slot, k].astype(f32)
+
+        pl.when(p.z > 0)(lambda: more(5, 0))
+        pl.when(p.z < 3)(lambda: more(7, 2))
 
     def drain(self):
-        for k in range(HOPS):
+        p = self.p
+        for k in (0, 1, 2, 3, 4, 6):
             self.wire(k).wait_send()
+        pl.when(p.z < 3)(lambda: self.wire(5).wait_send())
+        pl.when(p.z > 0)(lambda: self.wire(7).wait_send())
+        pl.when(jnp.logical_not(p.inner))(lambda: self.wire(8).wait_send())
 
 
 class Tally:
@@ -555,14 +660,18 @@
         self.slope[:, at] = g
         self.up_sums[:, at] = total(g.astype(f32))
 
-    def mlp_down(self, n=256):
-        def body(k):
-            at = ds(k * n, n, 128)
-            w = self.w_down[:, :, :, :, at].reshape(self.hidden, n)
-            value = self.mid[:, at] + (nn(self.act[...], w) + self.vecs[DB : DB + 1, at])
-            self.out[:, at] = value.astype(bf16)
-
-        loop(self.d // n, body)
+    def mlp_down(self):
+        m = self.rows // 2
+
+        def body(i):
+            at = ds(i * m, m)
+            value = self.mid[at, :] + self.vec(DB)
+            for k in range(self.hidden // self.d):
+                w = self.w_down[k // 2, k % 2].reshape(self.d, self.d)
+                value = value + nn(self.act[at, pl.ds(k * self.d, self.d)], w)
+            self.out[at, :] = value.astype(bf16)
+
+        loop(2, body)
 
     def grad_h2(self, j):
         m = self.rows // 2
@@ -689,6 +798,13 @@
         self.sums[T1 : T1 + 1, :] = jnp.where(self.sid == 1, sums[2], 0.0)
 
 
+def pack(r):
+    slab = r["s_small"]
+    rows = [r[f"vec{i}"][...].astype(f32) for i in range(10)]
+    rows = [jnp.pad(v, ((0, 0), (0, 128 - v.shape[1]))) for v in rows]
+    slab[...] = jnp.concatenate(rows + [jnp.zeros((5, 128), f32)], axis=0).astype(bf16)
+
+
 def kernel(outer, groups, names, *refs):
     r = dict(zip(names, refs, strict=True))
     p = Place(outer, groups)
@@ -745,12 +861,6 @@
         )
     xs = Rows(p, r["xp"], r["x"], r["x_send"], r["x_recv"])
     cs = Rows(p, r["cp"], r["cot"], r["c_send"], r["c_recv"])
-    last = len(gs)
-
-    def gather_tick(t):
-        for lag, act in enumerate(("z_start", "z_finish", "mid", "diag", "finish")):
-            if 0 <= t - lag < last:
-                getattr(gs[t - lag], act)()
 
     ss = []
 
@@ -758,9 +868,13 @@
         ss.append(Scatter(p, len(ss), part, bufs, out, r["s_send"], r["s_recv"]))
 
     def bufs(kind, i):
-        flat = kind == "flat"
         found = [r[f"{kind}_{name}"].at[i] for name in ("core", "r1", "r2", "q1", "q2")]
-        slot = stage.at[pl.ds(UP + i if i < nh else OUT, 1)] if flat else r[f"{kind}_zs"].at[i]
+        if kind == "flat":
+            slot = stage.at[pl.ds(UP + i if i < nh else OUT, 1)]
+        elif kind == "head":
+            slot = stage.at[pl.ds(QKV, 3), :, :, pl.ds(i * 256, 256)]
+        else:
+            slot = r["tall_zs"].at[i]
         return found + [slot, r[f"{kind}_zr"].at[i]]
 
     for i in range(n_down):
@@ -774,127 +888,126 @@
         outs = [r["o_qkv"].at[:, pl.ds(k * d + g * 256, 256)] for k in range(3)]
         give(w.at[pl.ds(QKV, 3), :, :, :, :, cols], bufs("head", g), outs)
 
-    def scatter_tick(t):
-        for lag, act in enumerate(("core_add", "pass_on", "z_start", "finish")):
-            if 0 <= t - lag < len(ss):
-                getattr(ss[t - lag], act)()
-
     ys = Rows(p, r["xp"], r["out"], r["y_send"], r["y_recv"])
-    ds_ = Rows(p, r["cp"], L.gx, r["d_send"], r["d_recv"])
+    rs = Rows(p, r["cp"], L.gx, r["d_send"], r["d_recv"])
     ts = Tally(p, r["value"], r["got"], r["t_send"], r["t_recv"])
 
+    ends = {X_IN: xs, C_IN: cs, Y_OUT: ys, R_OUT: rs}
+    gather = {SMALL: 0, WQ: 1, WK: 2, WV: 3, WO: 4, WU: 5, WD: 5 + nh}
+    scatter = {GD: 0, GU: n_down, GO: n_down + nh, GQ: n_down + nh + 1}
+    pairs = d // 128
+
+    def prepare():
+        for src, dst in ((r["patches"], r["xp"]), (r["cotangent"], r["cp"])):
+            dst[...] = jnp.zeros_like(dst)
+            for s in range(strips):
+                dst[s, :real] = src[s]
+        xs.in_local()
+        cs.in_local()
+
+    def sent():
+        for g in gs:
+            g.sent()
+        cs.in_sent()
+
+    def context_end():
+        for i in (pairs - 2, pairs - 1):
+            L.probs_out(i).wait()
+        L.mid_norm()
+
+    def rows_done():
+        L.back1()
+        r["sums"][10:16, :] = jnp.concatenate(
+            [L.up_sums[:, j * d : (j + 1) * d] for j in range(nh)]
+            + [jnp.zeros((6 - nh, d), f32)]
+        )
+        r["value"][0] = r["sums"][...]
+        ts.start()
+
+    def context_grad():
+        L.grad_ctx()
+        L.probs_in(0).start()
+
+    once = {
+        PREP: prepare, MASK: lambda: L.mask(r["lengths"], r["script_ids"], r["key_mask"]),
+        VEC: L.vectors, NORM1: L.norm1, MID: context_end, DOWN: L.mlp_down, BACK2: L.back2,
+        GCTX: context_grad, DWOUT: L.dw_out, BACK1: rows_done, SENT: sent,
+        SENTX: xs.in_sent,
+    }
+    counted = {
+        PROJ: L.project, UP_: L.mlp_up, GU_: L.grad_h2, DWUP: L.dw_up, GQ_: L.grad_h1,
+        DWQKV: L.dw_qkv, T: ts.step,
+    }
+    looped = {
+        ATT: L.attend, DWDOWN: L.dw_down, GPRE: L.grad_pre,
+        ATTB: lambda i: L.attend_back(i, pairs),
+    }
+
+    def act(step):
+        kind, name, i = step
+        if kind == ROW:
+            ends[name].in_start(i)
+        elif kind == IN:
+            ends[name].in_finish()
+        elif kind == OUT_:
+            ends[name].out_start()
+        elif name in gather:
+            g = gs[gather[name] + i]
+            {
+                ZS: g.z_start, ZF: g.z_far, ZE: g.z_end, FIN: g.finish,
+                MX: lambda: g.pass_on(3, 6, 8), MY: lambda: g.pass_on(4, 5, 9),
+                DX: lambda: g.pass_on(6, None, 10), DY: lambda: g.pass_on(5, None, 11),
+            }[kind]()
+        else:
+            s = ss[scatter[name] + i]
+            {
+                ST: s.start, CA: s.core_add, PX: s.pass_x, PY: s.pass_y, ZT: s.z_start,
+                ZP: s.z_pass, FI: s.finish,
+            }[kind]()
+
+    pack(r)
     p.greet()
-    gather_tick(0)
-    gather_tick(1)
-    for src, dst in ((r["patches"], r["xp"]), (r["cotangent"], r["cp"])):
-        dst[...] = jnp.zeros_like(dst)
-        for s in range(strips):
-            dst[s, :real] = src[s]
-    gather_tick(2)
-    xs.in_start()
-    L.mask(r["lengths"], r["script_ids"], r["key_mask"])
-    gather_tick(3)
-    gather_tick(4)
-    L.vectors()
-    xs.in_finish()
-    L.norm1()
-    gather_tick(5)
-    L.project(0)
-    gather_tick(6)
-    cs.in_start()
-    L.project(1)
-    gather_tick(7)
-    L.project(2)
-    gather_tick(8)
-    pairs = d // 128
-
-    def attend(i):
-        L.attend(i)
-        for k, t in ((1, 9), (3, 10)):
-
-            @pl.when(i == k)
-            def _():
-                gather_tick(t)
-
-    loop(pairs, attend)
-    for i in (pairs - 2, pairs - 1):
-        L.probs_out(i).wait()
-    L.mid_norm()
-    gather_tick(11)
-    for j in range(nh - 1):
-        L.mlp_up(j)
-    gather_tick(12)
-    L.mlp_up(nh - 1)
-    cs.in_finish()
-    xs.in_sent()
-    cs.in_sent()
-
-    def down(i):
-        L.dw_down(i)
-
-        @pl.when(i == 3)
-        def _():
-            gather_tick(13)
-
-    loop(8, down)
-    for i in range(n_down):
-        ss[i].start()
-    for t in range(14, last + 4):
-        gather_tick(t)
-    scatter_tick(0)
-
-    def grad_pre(i):
-        L.grad_pre(i)
-
-        @pl.when(i == 3)
-        def _():
-            scatter_tick(1)
-
-    loop(8, grad_pre)
-    scatter_tick(2)
-    for j in range(nh):
-        L.grad_h2(j)
-    for j in range(nh):
-        L.dw_up(j)
-        ss[n_down + j].start()
-        scatter_tick(n_down + j)
-    L.mlp_down()
-    ys.out_start()
-    L.back2()
-    L.grad_ctx()
-    L.dw_out()
-    at = n_down + nh
-    ss[at].start()
-    scatter_tick(at)
-    L.probs_in(0).start()
-    for g in range(d // 256):
-        loop(2, lambda i: L.attend_back(2 * g + i, pairs))
-        L.grad_h1(g)
-        L.dw_qkv(g)
-        at += 1
-        ss[at].start()
-        if g < d // 256 - 1:
-            scatter_tick(at)
-    L.back1()
-    ds_.out_start()
-    r["value"][0] = jnp.concatenate(
-        [r["sums"][0:10, :]]
-        + [L.up_sums[:, j * d : (j + 1) * d] for j in range(nh)]
-        + [jnp.zeros((6 - nh, d), f32)]
-    )
-    ts.start()
-    scatter_tick(at)
-    ts.step(0)
-    scatter_tick(at + 1)
-    ts.step(1)
-    scatter_tick(at + 2)
-    ts.step(2)
+    steps = list(SCHEDULE)
+    while steps:
+        kind, name, first = steps.pop(0)
+        if name:
+            act((kind, name, first))
+        elif kind in once:
+            once[kind]()
+        elif kind in counted:
+            counted[kind](first)
+        else:
+            n, between = 1, {}
+            while True:
+                k = 0
+                while k < len(steps) and steps[k][1]:
+                    k += 1
+                if k == len(steps) or steps[k] != (kind, 0, first + n):
+                    break
+                between[n - 1] = steps[:k]
+                steps = steps[k + 1 :]
+                n += 1
+
+            def body(i):
+                looped[kind](first + i)
+                for at, some in between.items():
+                    if some:
+
+                        @pl.when(i == at)
+                        def _():
+                            for step in some:
+                                act(step)
+
+            if n == 1:
+                body(0)
+            else:
+                loop(n, body)
+
     ys.out_finish()
     for s in range(strips):
         r["o_out_rows"][s] = r["xp"][s, :real]
     r["o_tally"][...] = ts.finish()
-    scatter_tick(at + 3)
-    ds_.out_finish()
+    rs.out_finish()
     for s in range(strips):
         r["o_grad_rows"][s] = r["cp"][s, :real]
     for s in ss:
@@ -911,7 +1024,7 @@
     pad_rows = round_up(part_rows, 16)
     rows = groups * pad_rows
     vectors = [norm1_gain, norm1_bias, q_bias, v_bias, attn_out_bias, norm2_gain, norm2_bias,
-               down_bias, script_table[0], script_table[1]]
+               down_bias]
     weights = [w_qkv, w_attn_out, w_up, w_down]
     if outer > 1:
         mates = [[g * outer + i for i in range(outer)] for g in range(8)]
@@ -924,22 +1037,17 @@
             return lax.dynamic_slice_in_dim(a, seq * n, n, axis=0)
 
         vectors = [widen(a) for a in vectors]
+        script_table = widen(script_table.T).T
         up_bias = widen(up_bias)
         weights = [widen(a) for a in weights]
-    c = vectors[0].shape[0]
-    small = jnp.concatenate(
-        [
-            jnp.pad(jnp.stack(vectors), ((0, 0), (0, 128 - c))),
-            jnp.pad(up_bias[None], ((0, 5), (0, 128 - up_bias.shape[0]))),
-        ]
-    )
+    vectors = [v[None] for v in vectors] + [script_table, up_bias[None]]
     vm = pl.BlockSpec(memory_space=pltpu.VMEM)
     sm = pl.BlockSpec(memory_space=pltpu.SMEM)
     anywhere = pl.BlockSpec(memory_space=pl.ANY)
     sems = pltpu.SemaphoreType.DMA
     nh = hidden // d
     u, r, nd, ng = d // 8, d // parts, d // 256, d // 256
-    ins = ["s_small", "s_qkv", "s_out", "s_up", "s_down", "patches", "cotangent", "key_mask",
+    ins = [f"vec{i}" for i in range(10)] + ["s_qkv", "s_out", "s_up", "s_down", "patches", "cotangent", "key_mask",
            "lengths", "script_ids"]
     outs = {
         "o_qkv": ((r, 3 * d), f32),
@@ -953,6 +1061,7 @@
     }
     scratch = {
         "small": ((8, groups, 16, 128), bf16),
+        "s_small": ((16, 128), bf16),
         "stage": ((4 + nh, groups, r, d), bf16),
         "w": ((4 + nh, 2, 2, 2, u, d), bf16),
         "w_down": ((2, 2, 2, hidden // 8, d), bf16),
@@ -991,9 +1100,9 @@
         scratch[f"{kind}_r2"] = ((count, k, 2, uu // 2, n), bf16)
         scratch[f"{kind}_q1"] = ((count, k, uu // 2, n), bf16)
         scratch[f"{kind}_q2"] = ((count, k, uu // 2, n), bf16)
-        if kind != "flat":
-            scratch[f"{kind}_zs"] = ((count, k, groups, rr, n), bf16)
-        scratch[f"{kind}_zr"] = ((count, groups - 1, k, rr, n), bf16)
+        if kind == "tall":
+            scratch["tall_zs"] = ((count, k, groups, rr, n), bf16)
+        scratch[f"{kind}_zr"] = ((count, groups, k, rr, n), bf16)
     n_gather = 5 + nh + nd
     n_scatter = nd + nh + 1 + ng
     semaphores = {
@@ -1003,30 +1112,29 @@
         "out_sem": (2,), "in_sem": (2,),
     }
     for name in "xcyd":
-        semaphores[f"{name}_send"] = (groups - 1,)
-        semaphores[f"{name}_recv"] = (groups - 1,)
+        shape = (groups - 1,) if name in "yd" else (d // 256, groups - 1)
+        semaphores[f"{name}_send"] = shape
+        semaphores[f"{name}_recv"] = shape
     names = ins + list(outs) + list(scratch) + list(semaphores)
 
     def body(*refs):
         refs = dict(zip(names, refs, strict=True))
         act = refs["act"]
-        refs["out"] = refs["h2"]
-        refs["gb"] = act.at[:, pl.ds(0, d)]
-        refs["gctx"] = act.at[:, pl.ds(d, d)]
-        refs["gx"] = act.at[:, pl.ds(2 * d, d)]
+        for k, name in enumerate(("out", "gb", "gctx", "gx")):
+            refs[name] = act.at[:, pl.ds(k * d, d)]
         kernel(outer, groups, list(refs), *refs.values())
 
     res = pl.pallas_call(
         body,
         out_shape=[jax.ShapeDtypeStruct(*s) for s in outs.values()],
-        in_specs=[vm] * 8 + [sm] * 2,
+        in_specs=[vm] * 17 + [sm] * 2,
         out_specs=[vm] * 7 + [anywhere],
         scratch_shapes=[pltpu.VMEM(*s) for s in scratch.values()]
         + [sems(s) for s in semaphores.values()],
         compiler_params=pltpu.CompilerParams(
             collective_id=0, has_side_effects=True, vmem_limit_bytes=63 * 2**20
         ),
-    )(small, *weights, patches, cotangent, key_mask, lengths, script_ids)
+    )(*vectors, *weights, patches, cotangent, key_mask, lengths, script_ids)
     shards = list(res[:4])
     tally = res[4]
     if outer > 1:
@@ -1040,15 +1148,44 @@
 
         shards = [narrow(a) for a in shards]
         tally = lax.psum(tally, "dp", axis_index_groups=mates)
+    n = d // (parts * outer)
+    m = hidden // (parts * outer)
+    passed = [res[5], res[6]] + (shards if outer == 1 else [])
+    closed = pl.pallas_call(
+        functools.partial(close, groups, nh),
+        out_shape=[jax.ShapeDtypeStruct((1, n), f32)] * 8
+        + [jax.ShapeDtypeStruct((2, n), f32), jax.ShapeDtypeStruct((1, m), f32)]
+        + [jax.ShapeDtypeStruct(a.shape, a.dtype) for a in passed],
+        in_specs=[vm] * (1 + len(passed)),
+        out_specs=[vm] * (10 + len(passed)),
+    )(tally, *passed)
+    vec = [v.reshape(n) for v in closed[:8]]
+    table, vup = closed[8], closed[9].reshape(m)
+    if outer == 1:
+        shards = closed[12:]
+    return (
+        closed[10], closed[11], vec[G1], vec[B1], shards[0], vec[QB], vec[VB], shards[1], vec[OB],
+        vec[G2], vec[B2], shards[2], vup, shards[3], vec[DB], table,
+    )
+
+
+def close(groups, nh, tally, *refs):
+    n_passed = (len(refs) - 10) // 2
+    passed, outs = refs[:n_passed], refs[n_passed:]
+    for src, dst in zip(passed, outs[10:], strict=True):
+        dst[...] = src[...]
     me = lax.axis_index("dp") * groups + lax.axis_index("seq")
-    n = d // (parts * outer)
-    vec = lax.dynamic_slice_in_dim(tally[:10], me * n, n, axis=1)
-    m = hidden // (parts * outer)
-    vup = lax.dynamic_slice_in_dim(tally[10 : 10 + nh].reshape(hidden), me * m, m, axis=0)
-    return (
-        res[5], res[6], vec[G1], vec[B1], shards[0], vec[QB], vec[VB], shards[1], vec[OB], vec[G2],
-        vec[B2], shards[2], vup, shards[3], vec[DB], vec[T0 : T1 + 1],
-    )
+    d = tally.shape[1]
+    n, m = outs[0].shape[1], outs[9].shape[1]
+    mine = pltpu.roll(tally[...], lax.rem(d - me * n, d), 1)
+    for i in range(8):
+        outs[i][...] = mine[i : i + 1, :n]
+    outs[8][...] = mine[T0 : T1 + 1, :n]
+    row = jnp.zeros((8, d), f32)
+    for i in range(nh):
+        line = jnp.broadcast_to(tally[10 + i : 11 + i, :], (8, d))
+        row = jnp.where(me * m // d == i, line, row)
+    outs[9][...] = pltpu.roll(row, lax.rem(d - lax.rem(me * m, d), d), 1)[0:1, :m]
 
 
 def solution(mesh):

time: 238 us -> 174 us (0.73)
  Pallas kernels: 219 us -> 174 us
  local copies, waits for them, and re-layouts: 16.2 us -> 0 us
    pallas_call x1, Pallas kernels: 219 us -> 171 us  [on_device(): pl.pallas_call(body, out_shape=[jax.ShapeDtypeStruct(*s) for s in outs.va...]
    unnamed x6 -> x0, local copies, waits for them, and re-layouts: 10.4 us -> none
    pallas_call x0 -> x1, Pallas kernels: none -> 2.98 us  [on_device(): pl.pallas_call(functools.partial(close, groups, nh), out_shape=[jax.Shape...]
where the time goes in v1:
time: 174 us
  Pallas kernels  174 us (100%)
    pallas_call x1, Pallas kernels, on_device(): pl.pallas_call(body, out_shape=[jax.ShapeDtypeStruct(*s) for s in outs.va...  171 us

profile of v1, /device:TPU:0, one launch (start us, length us, event | category | flops | bytes accessed | tf_op | source)
XLA Modules:
  0.0 174.2 jit_solution(1308236140835139394)
XLA Ops:
  0.7 170.6 %shard_map.306 = (f32[24,2304]{1,0:T(8,128)}, f32[24,768]{1,0:T(8,128)}, f32[24,3072]{1,0:T(8,128)}, f32[96,768]{1,0:T(8,128)}, f32[16,768]{1,0:T(8,128)}, /*ind...) custom-call(bf16[1,24]{1,0:T(2,128)(2,1)} %bitcast.18, ...), custom_call_target="tpu_custom_call" | custom-call | tf_op jit(solution)/shard_map/pallas_call | solution.py:1127
  171.2 3.0 %shard_map.307 = (f32[1,24]{1,0:T(1,128)}, f32[1,24]{1,0:T(1,128)}, f32[1,24]{1,0:T(1,128)}, f32[1,24]{1,0:T(1,128)}, f32[1,24]{1,0:T(1,128)}, /*index=5*/f32[1,...) custom-call(f32[16,768]{1,0:T(8,128)} %get-tuple-element.39.tally, ...), custom_call_target="tpu_custom_call" | custom-call | tf_op jit(solution)/shard_map/pallas_call | solution.py:1154

commit v2 on v1

--- a/solution.py
+++ b/solution.py
@@ -14,7 +14,7 @@
 epsilon = 1e-06
 WIRE = 13
 FAR = 12
-DIRECT = 1
+DIRECT = 2
 HOPS = 9
 QKV, OUT, UP = 0, 3, 4
 G1, B1, QB, VB, OB, G2, B2, DB, T0, T1 = range(10)
@@ -63,43 +63,43 @@
 (PREP, MASK, VEC, NORM1, PROJ, ATT, MID, UP_, DWDOWN, GPRE, DOWN, GU_, BACK2, GCTX, DWUP, ATTB,
  GQ_, DWQKV, BACK1, DWOUT, SENT, SENTX, T) = range(100, 123)
 SCHEDULE = (
-    (ZS, SMALL, 0), (ZS, WQ, 0), (ZS, WK, 0), (PREP, 0, 0), (ZS, WV, 0), (MASK, 0, 0),
-    (ZS, WO, 0), (ZE, SMALL, 0), (ZF, WQ, 0), (ROW, X_IN, 0), (MX, SMALL, 0), (MY, SMALL, 0),
-    (ZF, WK, 0), (DX, SMALL, 0), (DY, SMALL, 0), (ZF, WV, 0), (FIN, SMALL, 0), (VEC, 0, 0),
-    (ZF, WO, 0), (ZE, WQ, 0), (ZS, WU, 0), (ROW, X_IN, 1), (ZE, WK, 0), (ZE, WV, 0), (MX, WQ, 0),
-    (MY, WQ, 0), (ZE, WO, 0), (ZS, WU, 1), (ZF, WU, 0), (ROW, X_IN, 2), (MX, WK, 0), (MY, WK, 0),
-    (MX, WV, 0), (ZS, WU, 2), (MY, WV, 0), (ZF, WU, 1), (ZE, WU, 0), (DX, WQ, 0), (DY, WQ, 0),
-    (ZS, WU, 3), (ZS, WD, 0), (MX, WO, 0), (MY, WO, 0), (IN, X_IN, 0), (NORM1, 0, 0),
-    (ROW, C_IN, 0), (DX, WK, 0), (DY, WK, 0), (FIN, WQ, 0), (PROJ, 0, 0), (DX, WV, 0),
-    (DY, WV, 0), (ZE, WU, 1), (ZF, WU, 2), (FIN, WK, 0), (PROJ, 0, 1), (ZF, WU, 3), (FIN, WV, 0),
-    (PROJ, 0, 2), (MX, WU, 0), (MY, WU, 0), (ATT, 0, 0), (ZS, WD, 1), (DX, WO, 0), (DY, WO, 0),
-    (ZF, WD, 0), (ATT, 0, 1), (ROW, C_IN, 1), (MX, WU, 1), (MY, WU, 1), (ATT, 0, 2), (DX, WU, 0),
-    (DY, WU, 0), (ZE, WU, 2), (ZE, WU, 3), (ATT, 0, 3), (ZS, WD, 2), (DX, WU, 1), (DY, WU, 1),
-    (ZF, WD, 1), (ATT, 0, 4), (ZE, WD, 0), (ATT, 0, 5), (SENTX, 0, 0), (ROW, C_IN, 2),
-    (MX, WU, 2), (MY, WU, 2), (FIN, WO, 0), (MID, 0, 0), (MX, WU, 3), (MY, WU, 3), (FIN, WU, 0),
-    (UP_, 0, 0), (ZE, WD, 1), (ZF, WD, 2), (FIN, WU, 1), (UP_, 0, 1), (MX, WD, 0), (MY, WD, 0),
-    (DX, WU, 2), (DY, WU, 2), (FIN, WU, 2), (UP_, 0, 2), (DX, WU, 3), (DY, WU, 3), (ZE, WD, 2),
-    (FIN, WU, 3), (UP_, 0, 3), (IN, C_IN, 0), (DWDOWN, 0, 0), (MX, WD, 1), (MY, WD, 1),
-    (DWDOWN, 0, 1), (DWDOWN, 0, 2), (DWDOWN, 0, 3), (DX, WD, 0), (DY, WD, 0), (DWDOWN, 0, 4),
-    (DWDOWN, 0, 5), (DWDOWN, 0, 6), (DWDOWN, 0, 7), (ST, GD, 0), (ST, GD, 1), (ST, GD, 2),
-    (MX, WD, 2), (MY, WD, 2), (CA, GD, 0), (DX, WD, 1), (DY, WD, 1), (CA, GD, 1), (DX, WD, 2),
-    (DY, WD, 2), (CA, GD, 2), (FIN, WD, 0), (FIN, WD, 1), (FIN, WD, 2), (GPRE, 0, 0),
-    (GPRE, 0, 1), (GPRE, 0, 2), (GPRE, 0, 3), (PX, GD, 0), (PY, GD, 0), (GPRE, 0, 4),
-    (GPRE, 0, 5), (GPRE, 0, 6), (GPRE, 0, 7), (DOWN, 0, 0), (OUT_, Y_OUT, 0), (PX, GD, 1),
-    (PY, GD, 1), (GU_, 0, 0), (GU_, 0, 1), (PY, GD, 2), (PX, GD, 2), (GU_, 0, 2), (GU_, 0, 3),
-    (SENT, 0, 0), (DWUP, 0, 0), (ST, GU, 0), (ZT, GD, 0), (DWUP, 0, 1), (ST, GU, 1), (ZT, GD, 1),
-    (CA, GU, 0), (DWUP, 0, 2), (ST, GU, 2), (ZT, GD, 2), (CA, GU, 1), (DWUP, 0, 3), (ST, GU, 3),
-    (CA, GU, 2), (BACK2, 0, 0), (PX, GU, 0), (PY, GU, 0), (CA, GU, 3), (GCTX, 0, 0), (ATTB, 0, 0),
-    (PX, GU, 1), (PY, GU, 1), (ATTB, 0, 1), (ZP, GD, 0), (GQ_, 0, 0), (PX, GU, 2), (PY, GU, 2),
-    (DWQKV, 0, 0), (ST, GQ, 0), (ZP, GD, 1), (ZT, GU, 0), (ZP, GD, 2), (ATTB, 0, 2), (FI, GD, 0),
-    (PX, GU, 3), (PY, GU, 3), (CA, GQ, 0), (ATTB, 0, 3), (FI, GD, 1), (ZT, GU, 1), (GQ_, 0, 1),
-    (ZP, GU, 0), (ZT, GU, 2), (DWQKV, 0, 1), (ST, GQ, 1), (FI, GD, 2), (ZT, GU, 3), (ATTB, 0, 4),
-    (ZP, GU, 1), (FI, GU, 0), (PX, GQ, 0), (PY, GQ, 0), (CA, GQ, 1), (ATTB, 0, 5), (ZP, GU, 2),
-    (ZP, GU, 3), (GQ_, 0, 2), (BACK1, 0, 0), (OUT_, R_OUT, 0), (FI, GU, 1), (ZT, GQ, 0), (T, 0, 0),
-    (DWQKV, 0, 2), (ST, GQ, 2), (FI, GU, 2), (DWOUT, 0, 0), (ST, GO, 0), (T, 0, 1), (FI, GU, 3),
-    (PX, GQ, 1), (PY, GQ, 1), (CA, GQ, 2), (CA, GO, 0), (ZT, GQ, 1), (PY, GQ, 2), (T, 0, 2),
-    (PX, GQ, 2), (PY, GO, 0), (PX, GO, 0), (ZT, GQ, 2), (ZT, GO, 0), (ZP, GQ, 0), (ZP, GQ, 1),
-    (ZP, GQ, 2), (ZP, GO, 0), (FI, GQ, 0), (FI, GQ, 1), (FI, GQ, 2), (FI, GO, 0),
+    (ZS, SMALL, 0), (ZS, WK, 0), (PREP, 0, 0), (ZS, WV, 0), (MASK, 0, 0), (ZS, WQ, 0),
+    (ZE, SMALL, 0), (ZF, WK, 0), (ROW, X_IN, 0), (MX, SMALL, 0), (MY, SMALL, 0), (ZF, WV, 0),
+    (DX, SMALL, 0), (DY, SMALL, 0), (ZE, WQ, 0), (ZE, WK, 0), (ZS, WU, 2), (FIN, SMALL, 0),
+    (VEC, 0, 0), (ZS, WO, 0), (ROW, X_IN, 1), (ZE, WV, 0), (MX, WQ, 0), (MY, WQ, 0), (ZF, WU, 2),
+    (MX, WK, 0), (ZS, WU, 0), (MY, WK, 0), (ZF, WO, 0), (ROW, X_IN, 2), (MX, WV, 0), (MY, WV, 0),
+    (DX, WQ, 0), (DY, WQ, 0), (ZE, WU, 2), (DX, WK, 0), (DY, WK, 0), (ZF, WU, 0), (ZE, WO, 0),
+    (ZS, WU, 1), (DX, WV, 0), (DY, WV, 0), (ZS, WU, 3), (MX, WU, 2), (ZS, WD, 0), (MY, WU, 2),
+    (IN, X_IN, 0), (NORM1, 0, 0), (ZE, WU, 0), (FIN, WQ, 0), (PROJ, 0, 0), (ZS, WD, 2),
+    (MX, WO, 0), (MY, WO, 0), (ZF, WU, 1), (FIN, WK, 0), (PROJ, 0, 1), (DX, WU, 2), (DY, WU, 2),
+    (ZF, WU, 3), (FIN, WV, 0), (PROJ, 0, 2), (ROW, C_IN, 0), (ATT, 0, 0), (MX, WU, 0),
+    (MY, WU, 0), (ZF, WD, 0), (ATT, 0, 1), (DX, WO, 0), (DY, WO, 0), (ZE, WU, 1), (ZE, WU, 3),
+    (ZS, WD, 1), (ZF, WD, 2), (ATT, 0, 2), (DX, WU, 0), (DY, WU, 0), (ATT, 0, 3), (ROW, C_IN, 1),
+    (ATT, 0, 4), (MX, WU, 1), (MY, WU, 1), (ZE, WD, 0), (ATT, 0, 5), (SENTX, 0, 0),
+    (ROW, C_IN, 2), (MX, WU, 3), (MY, WU, 3), (ZF, WD, 1), (ZE, WD, 2), (FIN, WO, 0), (MID, 0, 0),
+    (DX, WU, 1), (DY, WU, 1), (FIN, WU, 0), (UP_, 0, 0), (FIN, WU, 1), (UP_, 0, 1), (MX, WD, 0),
+    (MY, WD, 0), (FIN, WU, 2), (UP_, 0, 2), (DX, WU, 3), (DY, WU, 3), (ZE, WD, 1), (FIN, WU, 3),
+    (UP_, 0, 3), (IN, C_IN, 0), (DWDOWN, 0, 0), (MX, WD, 2), (MY, WD, 2), (DWDOWN, 0, 1),
+    (DWDOWN, 0, 2), (DWDOWN, 0, 3), (DX, WD, 0), (DY, WD, 0), (DWDOWN, 0, 4), (DWDOWN, 0, 5),
+    (DWDOWN, 0, 6), (DWDOWN, 0, 7), (ST, GD, 0), (ST, GD, 1), (ST, GD, 2), (MX, WD, 1),
+    (MY, WD, 1), (CA, GD, 0), (DX, WD, 2), (DY, WD, 2), (CA, GD, 1), (CA, GD, 2), (DX, WD, 1),
+    (DY, WD, 1), (FIN, WD, 0), (FIN, WD, 1), (FIN, WD, 2), (GPRE, 0, 0), (GPRE, 0, 1),
+    (GPRE, 0, 2), (GPRE, 0, 3), (PX, GD, 0), (PY, GD, 0), (GPRE, 0, 4), (GPRE, 0, 5),
+    (GPRE, 0, 6), (DOWN, 0, 0), (OUT_, Y_OUT, 0), (PX, GD, 1), (PY, GD, 1), (GPRE, 0, 7),
+    (GU_, 0, 0), (SENT, 0, 0), (DWUP, 0, 0), (ST, GU, 0), (PX, GD, 2), (PY, GD, 2), (GU_, 0, 1),
+    (GU_, 0, 2), (ZT, GD, 0), (DWUP, 0, 2), (ST, GU, 2), (ZT, GD, 1), (CA, GU, 0), (GU_, 0, 3),
+    (BACK2, 0, 0), (ZT, GD, 2), (CA, GU, 2), (DWUP, 0, 1), (ST, GU, 1), (GCTX, 0, 0),
+    (ATTB, 0, 0), (PX, GU, 0), (PY, GU, 0), (CA, GU, 1), (ATTB, 0, 1), (PX, GU, 2), (PY, GU, 2),
+    (DWUP, 0, 3), (ST, GU, 3), (ZP, GD, 0), (GQ_, 0, 0), (ZT, GU, 0), (DWQKV, 0, 0), (ST, GQ, 0),
+    (ZP, GD, 1), (CA, GU, 3), (ATTB, 0, 2), (FI, GD, 0), (ZP, GD, 2), (PX, GU, 1), (PY, GU, 1),
+    (ZT, GU, 2), (CA, GQ, 0), (ATTB, 0, 3), (FI, GD, 1), (ZP, GU, 0), (ATTB, 0, 4), (FI, GD, 2),
+    (PX, GU, 3), (PY, GU, 3), (ZT, GU, 1), (ATTB, 0, 5), (FI, GU, 0), (ZP, GU, 2), (GQ_, 0, 1),
+    (PX, GQ, 0), (PY, GQ, 0), (DWQKV, 0, 1), (ST, GQ, 1), (ZP, GU, 1), (ZT, GU, 3), (GQ_, 0, 2),
+    (BACK1, 0, 0), (OUT_, R_OUT, 0), (FI, GU, 2), (CA, GQ, 1), (T, 0, 0), (ZT, GQ, 0),
+    (DWQKV, 0, 2), (ST, GQ, 2), (FI, GU, 1), (DWOUT, 0, 0), (T, 0, 1), (ST, GO, 0), (ZP, GU, 3),
+    (CA, GQ, 2), (CA, GO, 0), (PX, GQ, 1), (PY, GQ, 1), (PX, GQ, 2), (T, 0, 2), (PY, GQ, 2),
+    (PX, GO, 0), (PY, GO, 0), (ZT, GQ, 1), (ZT, GQ, 2), (ZT, GO, 0), (ZP, GQ, 0), (FI, GU, 3),
+    (ZP, GQ, 1), (ZP, GQ, 2), (ZP, GO, 0), (FI, GQ, 0), (FI, GQ, 1), (FI, GQ, 2), (FI, GO, 0),
 )
 
 
@@ -137,10 +137,10 @@
 
 
 class Gather:
-    def __init__(self, place, index, shard, block, part, land, send, recv, settle=None):
+    def __init__(self, place, index, shard, block, part, land, send, recv, here, settle=None):
         self.p, self.i, self.shard = place, index, shard
         self.block, self.part, self.land, self.settle = block, part, land, settle
-        self.send, self.recv = send, recv
+        self.send, self.recv, self.here = send, recv, here
 
     def copy(self, k, ref, to):
         return remote(ref, ref, self.send.at[self.i, k], self.recv.at[self.i, k], to)
@@ -158,6 +158,9 @@
             src, self.land(owner), self.send.at[self.i, k], self.recv.at[self.i, k], p.to_z(to)
         )
 
+    def own(self):
+        return pltpu.make_async_copy(self.shard, self.land(self.p.z), self.here.at[self.i])
+
     def z_got(self, k):
         z = self.p.z
         owner = ((z + 3) % 4, (z + 2) % 4, (z + 1) % 4)[k] if k < 3 else 3 - z
@@ -173,7 +176,7 @@
         pl.when(p.z > 0)(lambda: self.z_wire(2).start())
         if self.i < DIRECT:
             pl.when(jnp.logical_not(p.inner))(lambda: self.z_wire(FAR).start())
-        self.land(p.z)[...] = self.shard[...]
+        self.own().start()
 
     def z_far(self):
         if self.i < DIRECT:
@@ -209,6 +212,7 @@
 
     def z_end(self):
         p = self.p
+        self.own().wait()
         pl.when(p.z > 0)(lambda: self.z_got(0))
         pl.when(p.z < 3)(lambda: self.z_got(2))
 
@@ -311,6 +315,11 @@
             self.at(z), self.parts.at[s], self.send.at[j - 1], self.recv.at[j - 1], self.p.to_z(z)
         )
 
+    def stay(self, home):
+        return pltpu.make_async_copy(
+            self.at(self.p.z), self.parts.at[home], self.send.at[self.p.groups - 1]
+        )
+
     def out_start(self):
         p = self.p
 
@@ -319,7 +328,7 @@
             home = self.clip(self.home)
             for j in range(1, p.groups):
                 self.outward(j, home).start()
-            self.parts[home] = self.strip[ds(p.z * self.rows, self.rows), :]
+            self.stay(home).start()
 
     def out_finish(self):
         p = self.p
@@ -334,6 +343,7 @@
         def _():
             for j in range(1, p.groups):
                 self.outward(j, self.clip(self.home)).wait_send()
+            self.stay(self.clip(self.home)).wait()
 
 
 class Scatter:
@@ -822,7 +832,9 @@
 
     def add(shard, block, part, land, settle=None):
         gs.append(
-            Gather(p, len(gs), shard, block, part, land, r["g_send"], r["g_recv"], settle)
+            Gather(
+                p, len(gs), shard, block, part, land, r["g_send"], r["g_recv"], r["g_here"], settle
+            )
         )
 
     add(
@@ -888,8 +900,8 @@
         outs = [r["o_qkv"].at[:, pl.ds(k * d + g * 256, 256)] for k in range(3)]
         give(w.at[pl.ds(QKV, 3), :, :, :, :, cols], bufs("head", g), outs)
 
-    ys = Rows(p, r["xp"], r["out"], r["y_send"], r["y_recv"])
-    rs = Rows(p, r["cp"], L.gx, r["d_send"], r["d_recv"])
+    ys = Rows(p, r["o_out_rows"], r["out"], r["y_send"], r["y_recv"])
+    rs = Rows(p, r["o_grad_rows"], L.gx, r["d_send"], r["d_recv"])
     ts = Tally(p, r["value"], r["got"], r["t_send"], r["t_recv"])
 
     ends = {X_IN: xs, C_IN: cs, Y_OUT: ys, R_OUT: rs}
@@ -897,8 +909,16 @@
     scatter = {GD: 0, GU: n_down, GO: n_down + nh, GQ: n_down + nh + 1}
     pairs = d // 128
 
+    fetch = [
+        pltpu.make_async_copy(r[a], r[b], r["arg_sem"].at[i])
+        for i, (a, b) in enumerate((("patches", "pin"), ("cotangent", "cin")))
+    ]
+    for copy in fetch:
+        copy.start()
+
     def prepare():
-        for src, dst in ((r["patches"], r["xp"]), (r["cotangent"], r["cp"])):
+        for copy, src, dst in zip(fetch, (r["pin"], r["cin"]), (r["xp"], r["cp"]), strict=True):
+            copy.wait()
             dst[...] = jnp.zeros_like(dst)
             for s in range(strips):
                 dst[s, :real] = src[s]
@@ -1004,12 +1024,8 @@
                 loop(n, body)
 
     ys.out_finish()
-    for s in range(strips):
-        r["o_out_rows"][s] = r["xp"][s, :real]
     r["o_tally"][...] = ts.finish()
     rs.out_finish()
-    for s in range(strips):
-        r["o_grad_rows"][s] = r["cp"][s, :real]
     for s in ss:
         s.drain()
 
@@ -1055,8 +1071,8 @@
         "o_up": ((r, hidden), f32),
         "o_down": ((hidden // parts, d), f32),
         "o_tally": ((16, d), f32),
-        "o_out_rows": (patches.shape, bf16),
-        "o_grad_rows": (patches.shape, bf16),
+        "o_out_rows": ((strips, pad_rows, d), bf16),
+        "o_grad_rows": ((strips, pad_rows, d), bf16),
         "kept": ((d // 128, 2, rows, rows), bf16),
     }
     scratch = {
@@ -1066,6 +1082,8 @@
         "w": ((4 + nh, 2, 2, 2, u, d), bf16),
         "w_down": ((2, 2, 2, hidden // 8, d), bf16),
         "p_down": ((1, 2, 2, 2, hidden // 8, d), bf16),
+        "pin": (patches.shape, bf16),
+        "cin": (patches.shape, bf16),
         "xp": ((strips, pad_rows, d), bf16),
         "cp": ((strips, pad_rows, d), bf16),
         "x": ((rows, d), bf16),
@@ -1109,10 +1127,10 @@
         "g_send": (n_gather, WIRE), "g_recv": (n_gather, WIRE),
         "s_send": (n_scatter, HOPS), "s_recv": (n_scatter, HOPS),
         "t_send": (2 + groups,), "t_recv": (2 + groups,),
-        "out_sem": (2,), "in_sem": (2,),
+        "out_sem": (2,), "in_sem": (2,), "g_here": (n_gather,), "arg_sem": (2,),
     }
     for name in "xcyd":
-        shape = (groups - 1,) if name in "yd" else (d // 256, groups - 1)
+        shape = (groups,) if name in "yd" else (d // 256, groups - 1)
         semaphores[f"{name}_send"] = shape
         semaphores[f"{name}_recv"] = shape
     names = ins + list(outs) + list(scratch) + list(semaphores)
@@ -1127,8 +1145,8 @@
     res = pl.pallas_call(
         body,
         out_shape=[jax.ShapeDtypeStruct(*s) for s in outs.values()],
-        in_specs=[vm] * 17 + [sm] * 2,
-        out_specs=[vm] * 7 + [anywhere],
+        in_specs=[vm] * 10 + [anywhere] * 6 + [vm] + [sm] * 2,
+        out_specs=[vm] * 5 + [anywhere] * 3,
         scratch_shapes=[pltpu.VMEM(*s) for s in scratch.values()]
         + [sems(s) for s in semaphores.values()],
         compiler_params=pltpu.CompilerParams(
@@ -1151,11 +1169,12 @@
     n = d // (parts * outer)
     m = hidden // (parts * outer)
     passed = [res[5], res[6]] + (shards if outer == 1 else [])
+    shapes = [patches.shape] * 2 + [a.shape for a in passed[2:]]
     closed = pl.pallas_call(
         functools.partial(close, groups, nh),
         out_shape=[jax.ShapeDtypeStruct((1, n), f32)] * 8
         + [jax.ShapeDtypeStruct((2, n), f32), jax.ShapeDtypeStruct((1, m), f32)]
-        + [jax.ShapeDtypeStruct(a.shape, a.dtype) for a in passed],
+        + [jax.ShapeDtypeStruct(n, a.dtype) for n, a in zip(shapes, passed, strict=True)],
         in_specs=[vm] * (1 + len(passed)),
         out_specs=[vm] * (10 + len(passed)),
     )(tally, *passed)
@@ -1173,7 +1192,11 @@
     n_passed = (len(refs) - 10) // 2
     passed, outs = refs[:n_passed], refs[n_passed:]
     for src, dst in zip(passed, outs[10:], strict=True):
-        dst[...] = src[...]
+        if len(src.shape) == 3:
+            for s in range(src.shape[0]):
+                dst[s] = src[s, : dst.shape[1]]
+        else:
+            dst[...] = src[...]
     me = lax.axis_index("dp") * groups + lax.axis_index("seq")
     d = tally.shape[1]
     n, m = outs[0].shape[1], outs[9].shape[1]

time: 174 us -> 169 us (0.971)
  Pallas kernels: 174 us -> 168 us
    pallas_call x1, Pallas kernels: 171 us -> 165 us  [on_device(): pl.pallas_call(body, out_shape=[jax.ShapeDtypeStruct(*s) for s in outs.va...]
where the time goes in v2:
time: 169 us
  Pallas kernels  168 us (99%)
    pallas_call x1, Pallas kernels, on_device(): pl.pallas_call(body, out_shape=[jax.ShapeDtypeStruct(*s) for s in outs.va...  165 us

profile of v2, /device:TPU:0, one launch (start us, length us, event | category | flops | bytes accessed | tf_op | source)
XLA Modules:
  0.0 169.0 jit_solution(13213031273864140258)
XLA Ops:
  0.7 165.3 %shard_map.306 = (f32[24,2304]{1,0:T(8,128)}, f32[24,768]{1,0:T(8,128)}, f32[24,3072]{1,0:T(8,128)}, f32[96,768]{1,0:T(8,128)}, f32[16,768]{1,0:T(8,128)}, /*ind...) custom-call(bf16[1,24]{1,0:T(2,128)(2,1)} %bitcast.18, ...), custom_call_target="tpu_custom_call" | custom-call | tf_op jit(solution)/shard_map/pallas_call | solution.py:1145
  166.0 3.0 %shard_map.307 = (f32[1,24]{1,0:T(1,128)}, f32[1,24]{1,0:T(1,128)}, f32[1,24]{1,0:T(1,128)}, f32[1,24]{1,0:T(1,128)}, f32[1,24]{1,0:T(1,128)}, /*index=5*/f32[1,...) custom-call(f32[16,768]{1,0:T(8,128)} %get-tuple-element.39.tally, ...), custom_call_target="tpu_custom_call" | custom-call | tf_op jit(solution)/shard_map/pallas_call | solution.py:1173

commit v3 on v2

--- a/solution.py
+++ b/solution.py
@@ -64,42 +64,41 @@
  GQ_, DWQKV, BACK1, DWOUT, SENT, SENTX, T) = range(100, 123)
 SCHEDULE = (
     (ZS, SMALL, 0), (ZS, WK, 0), (PREP, 0, 0), (ZS, WV, 0), (MASK, 0, 0), (ZS, WQ, 0),
-    (ZE, SMALL, 0), (ZF, WK, 0), (ROW, X_IN, 0), (MX, SMALL, 0), (MY, SMALL, 0), (ZF, WV, 0),
-    (DX, SMALL, 0), (DY, SMALL, 0), (ZE, WQ, 0), (ZE, WK, 0), (ZS, WU, 2), (FIN, SMALL, 0),
-    (VEC, 0, 0), (ZS, WO, 0), (ROW, X_IN, 1), (ZE, WV, 0), (MX, WQ, 0), (MY, WQ, 0), (ZF, WU, 2),
-    (MX, WK, 0), (ZS, WU, 0), (MY, WK, 0), (ZF, WO, 0), (ROW, X_IN, 2), (MX, WV, 0), (MY, WV, 0),
-    (DX, WQ, 0), (DY, WQ, 0), (ZE, WU, 2), (DX, WK, 0), (DY, WK, 0), (ZF, WU, 0), (ZE, WO, 0),
-    (ZS, WU, 1), (DX, WV, 0), (DY, WV, 0), (ZS, WU, 3), (MX, WU, 2), (ZS, WD, 0), (MY, WU, 2),
-    (IN, X_IN, 0), (NORM1, 0, 0), (ZE, WU, 0), (FIN, WQ, 0), (PROJ, 0, 0), (ZS, WD, 2),
-    (MX, WO, 0), (MY, WO, 0), (ZF, WU, 1), (FIN, WK, 0), (PROJ, 0, 1), (DX, WU, 2), (DY, WU, 2),
-    (ZF, WU, 3), (FIN, WV, 0), (PROJ, 0, 2), (ROW, C_IN, 0), (ATT, 0, 0), (MX, WU, 0),
-    (MY, WU, 0), (ZF, WD, 0), (ATT, 0, 1), (DX, WO, 0), (DY, WO, 0), (ZE, WU, 1), (ZE, WU, 3),
-    (ZS, WD, 1), (ZF, WD, 2), (ATT, 0, 2), (DX, WU, 0), (DY, WU, 0), (ATT, 0, 3), (ROW, C_IN, 1),
-    (ATT, 0, 4), (MX, WU, 1), (MY, WU, 1), (ZE, WD, 0), (ATT, 0, 5), (SENTX, 0, 0),
-    (ROW, C_IN, 2), (MX, WU, 3), (MY, WU, 3), (ZF, WD, 1), (ZE, WD, 2), (FIN, WO, 0), (MID, 0, 0),
-    (DX, WU, 1), (DY, WU, 1), (FIN, WU, 0), (UP_, 0, 0), (FIN, WU, 1), (UP_, 0, 1), (MX, WD, 0),
-    (MY, WD, 0), (FIN, WU, 2), (UP_, 0, 2), (DX, WU, 3), (DY, WU, 3), (ZE, WD, 1), (FIN, WU, 3),
-    (UP_, 0, 3), (IN, C_IN, 0), (DWDOWN, 0, 0), (MX, WD, 2), (MY, WD, 2), (DWDOWN, 0, 1),
-    (DWDOWN, 0, 2), (DWDOWN, 0, 3), (DX, WD, 0), (DY, WD, 0), (DWDOWN, 0, 4), (DWDOWN, 0, 5),
-    (DWDOWN, 0, 6), (DWDOWN, 0, 7), (ST, GD, 0), (ST, GD, 1), (ST, GD, 2), (MX, WD, 1),
-    (MY, WD, 1), (CA, GD, 0), (DX, WD, 2), (DY, WD, 2), (CA, GD, 1), (CA, GD, 2), (DX, WD, 1),
-    (DY, WD, 1), (FIN, WD, 0), (FIN, WD, 1), (FIN, WD, 2), (GPRE, 0, 0), (GPRE, 0, 1),
-    (GPRE, 0, 2), (GPRE, 0, 3), (PX, GD, 0), (PY, GD, 0), (GPRE, 0, 4), (GPRE, 0, 5),
-    (GPRE, 0, 6), (DOWN, 0, 0), (OUT_, Y_OUT, 0), (PX, GD, 1), (PY, GD, 1), (GPRE, 0, 7),
-    (GU_, 0, 0), (SENT, 0, 0), (DWUP, 0, 0), (ST, GU, 0), (PX, GD, 2), (PY, GD, 2), (GU_, 0, 1),
-    (GU_, 0, 2), (ZT, GD, 0), (DWUP, 0, 2), (ST, GU, 2), (ZT, GD, 1), (CA, GU, 0), (GU_, 0, 3),
-    (BACK2, 0, 0), (ZT, GD, 2), (CA, GU, 2), (DWUP, 0, 1), (ST, GU, 1), (GCTX, 0, 0),
-    (ATTB, 0, 0), (PX, GU, 0), (PY, GU, 0), (CA, GU, 1), (ATTB, 0, 1), (PX, GU, 2), (PY, GU, 2),
-    (DWUP, 0, 3), (ST, GU, 3), (ZP, GD, 0), (GQ_, 0, 0), (ZT, GU, 0), (DWQKV, 0, 0), (ST, GQ, 0),
-    (ZP, GD, 1), (CA, GU, 3), (ATTB, 0, 2), (FI, GD, 0), (ZP, GD, 2), (PX, GU, 1), (PY, GU, 1),
-    (ZT, GU, 2), (CA, GQ, 0), (ATTB, 0, 3), (FI, GD, 1), (ZP, GU, 0), (ATTB, 0, 4), (FI, GD, 2),
-    (PX, GU, 3), (PY, GU, 3), (ZT, GU, 1), (ATTB, 0, 5), (FI, GU, 0), (ZP, GU, 2), (GQ_, 0, 1),
-    (PX, GQ, 0), (PY, GQ, 0), (DWQKV, 0, 1), (ST, GQ, 1), (ZP, GU, 1), (ZT, GU, 3), (GQ_, 0, 2),
-    (BACK1, 0, 0), (OUT_, R_OUT, 0), (FI, GU, 2), (CA, GQ, 1), (T, 0, 0), (ZT, GQ, 0),
-    (DWQKV, 0, 2), (ST, GQ, 2), (FI, GU, 1), (DWOUT, 0, 0), (T, 0, 1), (ST, GO, 0), (ZP, GU, 3),
-    (CA, GQ, 2), (CA, GO, 0), (PX, GQ, 1), (PY, GQ, 1), (PX, GQ, 2), (T, 0, 2), (PY, GQ, 2),
-    (PX, GO, 0), (PY, GO, 0), (ZT, GQ, 1), (ZT, GQ, 2), (ZT, GO, 0), (ZP, GQ, 0), (FI, GU, 3),
-    (ZP, GQ, 1), (ZP, GQ, 2), (ZP, GO, 0), (FI, GQ, 0), (FI, GQ, 1), (FI, GQ, 2), (FI, GO, 0),
+    (ZE, SMALL, 0), (ZS, WU, 1), (ZF, WK, 0), (ZS, WU, 3), (MX, SMALL, 0), (MY, SMALL, 0),
+    (ZF, WV, 0), (ZS, WO, 0), (ZE, WQ, 0), (DX, SMALL, 0), (DY, SMALL, 0), (ROW, X_IN, 0),
+    (ZF, WU, 1), (FIN, SMALL, 0), (VEC, 0, 0), (ZE, WK, 0), (ZF, WU, 3), (ZE, WV, 0), (ZS, WU, 0),
+    (MX, WQ, 0), (MY, WQ, 0), (ZF, WO, 0), (ROW, X_IN, 1), (MX, WK, 0), (MY, WK, 0), (ZE, WU, 1),
+    (ZE, WU, 3), (MX, WV, 0), (MY, WV, 0), (ZS, WU, 2), (ZF, WU, 0), (DX, WQ, 0), (DY, WQ, 0),
+    (ZE, WO, 0), (ROW, X_IN, 2), (DX, WK, 0), (DY, WK, 0), (MX, WU, 1), (MY, WU, 1), (ZS, WD, 2),
+    (ZF, WU, 2), (ZE, WU, 0), (MX, WU, 3), (MY, WU, 3), (ZS, WD, 1), (DX, WV, 0), (DY, WV, 0),
+    (ZS, WD, 0), (IN, X_IN, 0), (NORM1, 0, 0), (MX, WO, 0), (MY, WO, 0), (FIN, WQ, 0),
+    (PROJ, 0, 0), (DX, WU, 1), (DY, WU, 1), (ZF, WD, 2), (FIN, WK, 0), (PROJ, 0, 1),
+    (ROW, C_IN, 0), (ZE, WU, 2), (FIN, WV, 0), (PROJ, 0, 2), (ATT, 0, 0), (MX, WU, 0),
+    (MY, WU, 0), (ZF, WD, 1), (ATT, 0, 1), (ROW, C_IN, 1), (DY, WO, 0), (DX, WO, 0), (DX, WU, 3),
+    (DY, WU, 3), (ZF, WD, 0), (ZE, WD, 2), (ATT, 0, 2), (ATT, 0, 3), (MX, WU, 2), (MY, WU, 2),
+    (ATT, 0, 4), (SENTX, 0, 0), (ROW, C_IN, 2), (DX, WU, 0), (DY, WU, 0), (ZE, WD, 1),
+    (ATT, 0, 5), (FIN, WO, 0), (MID, 0, 0), (DX, WU, 2), (DY, WU, 2), (ZE, WD, 0), (MX, WD, 2),
+    (MY, WD, 2), (FIN, WU, 0), (UP_, 0, 0), (FIN, WU, 1), (UP_, 0, 1), (FIN, WU, 2), (UP_, 0, 2),
+    (MX, WD, 1), (MY, WD, 1), (FIN, WU, 3), (UP_, 0, 3), (IN, C_IN, 0), (DWDOWN, 0, 0),
+    (DWDOWN, 0, 1), (DWDOWN, 0, 2), (MX, WD, 0), (MY, WD, 0), (DWDOWN, 0, 3), (ST, GD, 0),
+    (ST, GD, 1), (ST, GD, 2), (DX, WD, 2), (DY, WD, 2), (DX, WD, 1), (DY, WD, 1), (CA, GD, 0),
+    (DX, WD, 0), (DY, WD, 0), (CA, GD, 1), (CA, GD, 2), (FIN, WD, 0), (FIN, WD, 1), (FIN, WD, 2),
+    (GPRE, 0, 0), (GPRE, 0, 1), (GPRE, 0, 2), (DOWN, 0, 0), (OUT_, Y_OUT, 0), (PX, GD, 0),
+    (PY, GD, 0), (GPRE, 0, 3), (PX, GD, 1), (PY, GD, 1), (GU_, 0, 0), (GU_, 0, 1), (GU_, 0, 2),
+    (SENT, 0, 0), (DWUP, 0, 2), (ST, GU, 2), (GU_, 0, 3), (PX, GD, 2), (PY, GD, 2), (DWUP, 0, 0),
+    (ST, GU, 0), (BACK2, 0, 0), (ZT, GD, 0), (CA, GU, 2), (GCTX, 0, 0), (ZT, GD, 1), (CA, GU, 0),
+    (DWUP, 0, 3), (ST, GU, 3), (ATTB, 0, 0), (ZT, GD, 2), (DWUP, 0, 1), (ST, GU, 1), (CA, GU, 3),
+    (ATTB, 0, 1), (PX, GU, 2), (PY, GU, 2), (ATTB, 0, 2), (PX, GU, 0), (PY, GU, 0), (CA, GU, 1),
+    (GQ_, 0, 0), (ZP, GD, 0), (DWQKV, 0, 0), (ST, GQ, 0), (ZP, GD, 1), (PX, GU, 3), (PY, GU, 3),
+    (ATTB, 0, 3), (ZP, GD, 2), (ZT, GU, 2), (ATTB, 0, 4), (FI, GD, 0), (ZT, GU, 0), (CA, GQ, 0),
+    (GQ_, 0, 1), (FI, GD, 1), (ATTB, 0, 5), (FI, GD, 2), (PX, GU, 1), (PY, GU, 1), (ZT, GU, 3),
+    (GQ_, 0, 2), (ZP, GU, 2), (DWQKV, 0, 2), (ST, GQ, 2), (ZP, GU, 0), (BACK1, 0, 0),
+    (OUT_, R_OUT, 0), (PX, GQ, 0), (PY, GQ, 0), (T, 0, 0), (DWOUT, 0, 0), (ST, GO, 0), (ZT, GU, 1),
+    (ZP, GU, 3), (CA, GQ, 2), (T, 0, 1), (DWQKV, 0, 1), (ST, GQ, 1), (FI, GU, 0), (FI, GU, 2),
+    (CA, GO, 0), (ZT, GQ, 0), (CA, GQ, 1), (T, 0, 2), (PX, GQ, 2), (PY, GQ, 2), (PX, GO, 0),
+    (PY, GO, 0), (PX, GQ, 1), (PY, GQ, 1), (ZT, GQ, 2), (ZT, GO, 0), (ZP, GU, 1), (ZT, GQ, 1),
+    (FI, GU, 3), (ZP, GQ, 0), (ZP, GQ, 2), (ZP, GO, 0), (FI, GU, 1), (ZP, GQ, 1), (FI, GQ, 0),
+    (FI, GQ, 2), (FI, GO, 0), (FI, GQ, 1),
 )
 
 
@@ -574,7 +573,7 @@
 
         loop(self.rows // self.step, body)
 
-    def project(self, i, n=256):
+    def project(self, i, n=768):
         d = self.d
 
         def body(k):
@@ -610,6 +609,7 @@
         q = self.qkv[:, aq] * jnp.asarray(DH**-0.5, bf16)
         k, v = self.qkv[:, ak], self.qkv[:, av]
         valid = self.valid[...] > 0
+        turned = v.T
 
         @pl.when(p >= 2)
         def _():
@@ -622,11 +622,11 @@
             e = jnp.exp(s - jnp.max(s, axis=0, keepdims=True))
             probs = (e * (1.0 / total(e))).astype(bf16)
             self.probs[p % 2, h] = probs
-            contexts.append(tn(probs, v))
-        self.ctx[:, ds(p * 128, 128, 128)] = self.pick(*contexts).astype(bf16)
+            contexts.append(nn(turned[h * DH : (h + 1) * DH], probs))
+        self.ctx[:, ds(p * 128, 128, 128)] = jnp.concatenate(contexts, axis=0).T.astype(bf16)
         self.probs_out(p).start()
 
-    def mid_norm(self, n=256):
+    def mid_norm(self, n=768):
         def body(k):
             at = ds(k * n, n, 128)
             self.mid[:, at] = nn(self.ctx[...], self.weight(OUT, at))
@@ -644,7 +644,7 @@
 
         loop(self.rows // self.step, norm)
 
-    def mlp_up(self, j, n=256):
+    def mlp_up(self, j, n=768):
         def body(k):
             at = ds(j * self.d + k * n, n, 128)
             pre = nn(self.h2[...], self.weight(UP + j, ds(k * n, n, 128))) + self.b_up[:, at]
@@ -655,18 +655,16 @@
 
         loop(self.d // n, body)
 
-    def down(self, b):
-        return self.w_down.at[b // 4, (b // 2) % 2, b % 2]
-
     def dw_down(self, b):
-        u = self.hidden // 8
+        u = self.hidden // 4
         grad = tn(self.act[:, ds(b * u, u, 128)], self.cot[...])
-        self.p_down[0, b // 4, (b // 2) % 2, b % 2] = grad.astype(bf16)
+        self.p_down[0, b // 2, b % 2] = grad.reshape(2, u // 2, self.d).astype(bf16)
 
     def grad_pre(self, b):
-        u = self.hidden // 8
+        u = self.hidden // 4
         at = ds(b * u, u, 128)
-        g = (nt(self.cot[...], self.down(b)[...]) * self.slope[:, at].astype(f32)).astype(bf16)
+        w = self.w_down[b // 2, b % 2].reshape(u, self.d)
+        g = (nt(self.cot[...], w) * self.slope[:, at].astype(f32)).astype(bf16)
         self.slope[:, at] = g
         self.up_sums[:, at] = total(g.astype(f32))
 
@@ -696,7 +694,7 @@
 
         loop(2, body)
 
-    def dw_up(self, j, n=256):
+    def dw_up(self, j, n=768):
         def body(k):
             grad = tn(self.h2[...], self.slope[:, ds(j * self.d + k * n, n, 128)])
             self.w[UP + j, :, :, :, :, ds(k * n, n, 128)] = self.eighths(grad).astype(bf16)
@@ -732,7 +730,7 @@
 
         loop(2, body)
 
-    def dw_out(self, n=256):
+    def dw_out(self, n=768):
         def body(k):
             at = ds(k * n, n, 128)
             grad = tn(self.ctx[...], self.gb[:, at])
@@ -750,6 +748,7 @@
             self.probs_in(p + 1).start()
 
         self.probs_in(p).wait()
+        turned = k.T
         dq, dk, dv = [], [], []
         for h in range(2):
             probs = self.probs[p % 2, h]
@@ -758,8 +757,8 @@
             wide = probs.astype(f32)
             grad = (wide * (grad - total(wide * grad))).astype(bf16)
             dk.append(nn(grad, q))
-            dq.append(tn(grad, k))
-        dq = (self.pick(*dq) * DH**-0.5).astype(bf16)
+            dq.append(nn(turned[h * DH : (h + 1) * DH], grad))
+        dq = (jnp.concatenate(dq, axis=0).T * DH**-0.5).astype(bf16)
         dv = self.pick(*dv).astype(bf16)
         self.qkv[:, aq] = dq
         self.qkv[:, ak] = (self.pick(*dk) * DH**-0.5).astype(bf16)
@@ -910,19 +909,26 @@
     pairs = d // 128
 
     fetch = [
-        pltpu.make_async_copy(r[a], r[b], r["arg_sem"].at[i])
-        for i, (a, b) in enumerate((("patches", "pin"), ("cotangent", "cin")))
+        pltpu.make_async_copy(r[a], r["pin"], r["arg_sem"].at[i])
+        for i, a in enumerate(("patches", "cotangent"))
     ]
-    for copy in fetch:
-        copy.start()
+    fetch[0].start()
+
+    def lay(dst):
+        dst[...] = jnp.zeros_like(dst)
+        for s in range(strips):
+            dst[s, :real] = r["pin"][s]
 
     def prepare():
-        for copy, src, dst in zip(fetch, (r["pin"], r["cin"]), (r["xp"], r["cp"]), strict=True):
-            copy.wait()
-            dst[...] = jnp.zeros_like(dst)
-            for s in range(strips):
-                dst[s, :real] = src[s]
+        fetch[0].wait()
+        lay(r["xp"])
+        fetch[1].start()
         xs.in_local()
+
+    def mask():
+        L.mask(r["lengths"], r["script_ids"], r["key_mask"])
+        fetch[1].wait()
+        lay(r["cp"])
         cs.in_local()
 
     def sent():
@@ -949,7 +955,7 @@
         L.probs_in(0).start()
 
     once = {
-        PREP: prepare, MASK: lambda: L.mask(r["lengths"], r["script_ids"], r["key_mask"]),
+        PREP: prepare, MASK: mask,
         VEC: L.vectors, NORM1: L.norm1, MID: context_end, DOWN: L.mlp_down, BACK2: L.back2,
         GCTX: context_grad, DWOUT: L.dw_out, BACK1: rows_done, SENT: sent,
         SENTX: xs.in_sent,
@@ -1083,7 +1089,6 @@
         "w_down": ((2, 2, 2, hidden // 8, d), bf16),
         "p_down": ((1, 2, 2, 2, hidden // 8, d), bf16),
         "pin": (patches.shape, bf16),
-        "cin": (patches.shape, bf16),
         "xp": ((strips, pad_rows, d), bf16),
         "cp": ((strips, pad_rows, d), bf16),
         "x": ((rows, d), bf16),

time: 169 us -> 169 us (level); the launches traced: 169 us -> 166 us
  Pallas kernels: 168 us -> 165 us
    pallas_call x1, Pallas kernels: 165 us -> 162 us  [on_device(): pl.pallas_call(body, out_shape=[jax.ShapeDtypeStruct(*s) for s in outs.va...]
where the time goes in v3:
time: 169 us; the launch traced here: 166 us
  Pallas kernels  165 us (98%)
    pallas_call x1, Pallas kernels, on_device(): pl.pallas_call(body, out_shape=[jax.ShapeDtypeStruct(*s) for s in outs.va...  162 us

profile of v3, /device:TPU:0, one launch (start us, length us, event | category | flops | bytes accessed | tf_op | source)
XLA Modules:
  0.0 166.1 jit_solution(6181136369805448476)
XLA Ops:
  0.7 162.2 %shard_map.306 = (f32[24,2304]{1,0:T(8,128)}, f32[24,768]{1,0:T(8,128)}, f32[24,3072]{1,0:T(8,128)}, f32[96,768]{1,0:T(8,128)}, f32[16,768]{1,0:T(8,128)}, /*ind...) custom-call(bf16[1,24]{1,0:T(2,128)(2,1)} %bitcast.18, ...), custom_call_target="tpu_custom_call" | custom-call | tf_op jit(solution)/shard_map/pallas_call | solution.py:1150
  162.8 3.0 %shard_map.307 = (f32[1,24]{1,0:T(1,128)}, f32[1,24]{1,0:T(1,128)}, f32[1,24]{1,0:T(1,128)}, f32[1,24]{1,0:T(1,128)}, f32[1,24]{1,0:T(1,128)}, /*index=5*/f32[1,...) custom-call(f32[16,768]{1,0:T(8,128)} %get-tuple-element.39.tally, ...), custom_call_target="tpu_custom_call" | custom-call | tf_op jit(solution)/shard_map/pallas_call | solution.py:1178

commit v4 on v3

--- a/solution.py
+++ b/solution.py
@@ -682,7 +682,7 @@
         loop(2, body)
 
     def grad_h2(self, j):
-        m = self.rows // 2
+        m = self.rows
 
         def body(i):
             at = ds(i * m, m)
@@ -692,7 +692,7 @@
             else:
                 self.wide[at, :] += value
 
-        loop(2, body)
+        loop(1, body)
 
     def dw_up(self, j, n=768):
         def body(k):
@@ -722,13 +722,13 @@
             self.sums[row : row + 1, :] = s
 
     def grad_ctx(self):
-        m = self.rows // 2
+        m = self.rows
 
         def body(i):
             at = ds(i * m, m)
             self.gctx[at, :] = nt(self.gb[at, :], self.weight(OUT)).astype(bf16)
 
-        loop(2, body)
+        loop(1, body)
 
     def dw_out(self, n=768):
         def body(k):

time: 169 us -> 169 us (level)
  no operation moved by 1% of the time
where the time goes in v4:
time: 169 us; the launch traced here: 166 us
  Pallas kernels  165 us (98%)
    pallas_call x1, Pallas kernels, on_device(): pl.pallas_call(body, out_shape=[jax.ShapeDtypeStruct(*s) for s in outs.va...  162 us

profile of v4, /device:TPU:0, one launch (start us, length us, event | category | flops | bytes accessed | tf_op | source)
XLA Modules:
  0.0 166.4 jit_solution(12554757257012016744)
XLA Ops:
  0.7 162.4 %shard_map.306 = (f32[24,2304]{1,0:T(8,128)}, f32[24,768]{1,0:T(8,128)}, f32[24,3072]{1,0:T(8,128)}, f32[96,768]{1,0:T(8,128)}, f32[16,768]{1,0:T(8,128)}, /*ind...) custom-call(bf16[1,24]{1,0:T(2,128)(2,1)} %bitcast.18, ...), custom_call_target="tpu_custom_call" | custom-call | tf_op jit(solution)/shard_map/pallas_call | solution.py:1150
  163.1 3.0 %shard_map.307 = (f32[1,24]{1,0:T(1,128)}, f32[1,24]{1,0:T(1,128)}, f32[1,24]{1,0:T(1,128)}, f32[1,24]{1,0:T(1,128)}, f32[1,24]{1,0:T(1,128)}, /*index=5*/f32[1,...) custom-call(f32[16,768]{1,0:T(8,128)} %get-tuple-element.39.tally, ...), custom_call_target="tpu_custom_call" | custom-call | tf_op jit(solution)/shard_map/pallas_call | solution.py:1178
